TPU v7x, 128 devices: a whole 4x4x4 slice. The times are simulated.
128 devices in a mesh: occ: 16 (over x, y), vir: 8 (over z, core).
Axes of the slice: x: 4, y: 4, z: 4, core: 2. Of those that a mesh axis runs over, the one named last changes fastest.
Arguments:
- t_tiles: bfloat16 [16384, 9216], P(('occ', 'vir')), may hold values from -6 to 6
- t_index: int32 [16384, 3], P(('occ', 'vir')), may hold values from 0 to 255, as said below
- cycle_map: int32 [256], replicated, may hold values from 0 to 15, as said below
- ladder_slots: int32 [3072, 3], P('occ'), may hold values from 0 to 47, as said below
- cycle_slots: int32 [3072, 3], P('occ'), may hold values from 0 to 47, as said below
- x_ints: bfloat16 [4608, 4608], P('occ', 'vir'), may hold values from -0.375 to 0.375
- y_ints: bfloat16 [4608, 4608], P('vir', 'occ'), may hold values from -0.375 to 0.375
Outputs:
- ladder_resid: float32 [3072, 9216], P(('occ', 'vir'))
- cycle_resid: float32 [3072, 9216], P(('occ', 'vir'))
Inputs may be any that keep to these rules, and one draw needn't show every extreme that they name: `t_index`: tile k on device (o, v) has p_k in o * 16 to o * 16 + 15 and c_k in v * 6 to v * 6 + 5; no two tiles share (p, c, d). Each pair has a domain of 8 virtual tiles, and its tiles are exactly those with c and d both in its domain. Taking a tile's cycle owner as the device (cycle_map[p_k], d_k // 6), every device holds at most 4 tiles for one cycle owner, and exactly 4 for some owner. For each group g and local index s exactly one o has cycle_map[o * 16 + s] = g, so the 16 pairs of one occ group go to 16 different groups. `ladder_slots`: the first entry of a row is below 16; a and b lie in the domain of the row's pair. `cycle_slots`: the first entry of a row is below 16; a and b lie in the domain of the row's pair.
All inputs are finite; a program needn't handle non-finite values.
Results may differ from a plain program's by a relative error of at most 0.012.
Values may be sent and summed in bfloat16 or wider, within the bound.
A program may use at most 128 MiB of HBM per device.

v0:
```python
import jax
import jax.numpy as jnp
from jax import lax
from jax.sharding import PartitionSpec as P

TILE = 96
NV = 48
CAP = 4


def blockwise(term, block_rows, row_count):
    firsts = block_rows * jnp.arange(row_count // block_rows, dtype=jnp.int32)
    pieces = lax.map(lambda block_first: term(block_first, block_rows), firsts)
    return pieces.reshape(row_count, -1)


def select_rows(table, wanted):
    ids = jnp.arange(table.shape[0], dtype=jnp.int32)
    onehot = (wanted[:, None] == ids[None, :]).astype(table.dtype)
    return jnp.dot(onehot, table, preferred_element_type=jnp.float32).astype(table.dtype)


def pick_tiles(tiles, matches):
    flat = matches.reshape(-1, matches.shape[-1]).astype(tiles.dtype)
    chosen = jnp.dot(flat, tiles, preferred_element_type=jnp.float32).astype(tiles.dtype)
    return chosen.reshape(matches.shape[0], matches.shape[1], TILE, TILE)


def on_device(t_tiles, t_index, cycle_map, ladder_slots, cycle_slots, x_ints, y_ints):
    occ_count = lax.axis_size("occ")
    vir_count = lax.axis_size("vir")
    occ_pos = lax.axis_index("occ")
    vir_pos = lax.axis_index("vir")
    device_count = occ_count * vir_count
    vir_tiles = NV // vir_count
    tile_area = TILE * TILE
    block_rows = ladder_slots.shape[0] // vir_count
    capacity = CAP
    tile_pairs = t_index[:, 0]
    tile_first = t_index[:, 1]
    tile_second = t_index[:, 2]
    local_range = jnp.arange(vir_tiles, dtype=jnp.int32)
    x_rows = lax.all_gather(x_ints, "occ", axis=0, tiled=True)
    x_table = (
        x_rows.reshape(NV, TILE, vir_tiles, TILE)
        .transpose(0, 2, 1, 3)
        .reshape(NV, vir_tiles * tile_area)
    )
    first_local = tile_first - vir_pos * vir_tiles

    def ladder_term(block_first, row_count):
        slot_rows = lax.dynamic_slice_in_dim(ladder_slots, block_first, row_count, 0)
        slot_pairs = occ_pos * occ_count + slot_rows[:, 0]
        matches = (
            (slot_pairs[:, None, None] == tile_pairs[None, None, :])
            & (slot_rows[:, 2][:, None, None] == tile_second[None, None, :])
            & (local_range[None, :, None] == first_local[None, None, :])
        )
        picked = pick_tiles(t_tiles, matches)
        x_picked = select_rows(x_table, slot_rows[:, 1]).reshape(row_count, vir_tiles, TILE, TILE)
        result = jnp.einsum("rcxy,rcyz->rxz", x_picked, picked, preferred_element_type=jnp.float32)
        return result.reshape(row_count, tile_area)

    owner_device = jnp.take(cycle_map, tile_pairs) * vir_count + tile_second // vir_tiles
    owner_marks = (
        owner_device[:, None] == jnp.arange(device_count, dtype=jnp.int32)[None, :]
    ).astype(jnp.int32)
    earlier = jnp.cumsum(owner_marks, axis=0) - owner_marks
    position = owner_device * capacity + jnp.sum(earlier * owner_marks, axis=1)
    send_tiles = (
        jnp.zeros((device_count * capacity, tile_area), t_tiles.dtype).at[position].set(t_tiles)
    )
    send_labels = jnp.full((device_count * capacity, 3), -1, jnp.int32).at[position].set(t_index)
    got_tiles, got_labels = (
        lax.all_to_all(
            send_tiles.reshape(device_count, capacity, tile_area),
            ("occ", "vir"),
            split_axis=0,
            concat_axis=0,
            tiled=True,
        ),
        lax.all_to_all(
            send_labels.reshape(device_count, capacity, 3),
            ("occ", "vir"),
            split_axis=0,
            concat_axis=0,
            tiled=True,
        ),
    )
    got_tiles = got_tiles.reshape(-1, tile_area)
    got_labels = got_labels.reshape(-1, 3)
    got_pairs = got_labels[:, 0]
    got_first = got_labels[:, 1]
    got_local = got_labels[:, 2] - vir_pos * vir_tiles
    y_rows = lax.all_gather(y_ints, "occ", axis=1, tiled=True)
    y_table = (
        y_rows.reshape(vir_tiles, TILE, NV, TILE)
        .transpose(2, 0, 1, 3)
        .reshape(NV, vir_tiles * tile_area)
    )
    owner_table = cycle_map.reshape(occ_count, occ_count)
    group_range = jnp.arange(occ_count, dtype=jnp.int32)
    pair_range = jnp.arange(occ_count, dtype=jnp.int32)
    owner_group = jnp.sum(jnp.where(owner_table == occ_pos, group_range[:, None], 0), axis=0)
    cycle_pairs = owner_group * occ_count + pair_range

    def cycle_term(block_first, row_count):
        slot_rows = lax.dynamic_slice_in_dim(cycle_slots, block_first, row_count, 0)
        slot_pairs = jnp.sum(
            jnp.where(slot_rows[:, 0][:, None] == pair_range[None, :], cycle_pairs[None, :], 0),
            axis=1,
        )
        matches = (
            (slot_pairs[:, None, None] == got_pairs[None, None, :])
            & (slot_rows[:, 1][:, None, None] == got_first[None, None, :])
            & (local_range[None, :, None] == got_local[None, None, :])
        )
        picked = pick_tiles(got_tiles, matches)
        y_picked = select_rows(y_table, slot_rows[:, 2]).reshape(row_count, vir_tiles, TILE, TILE)
        result = jnp.einsum("rcxy,rcyz->rxz", picked, y_picked, preferred_element_type=jnp.float32)
        return result.reshape(row_count, tile_area)

    ladder_resid = lax.psum_scatter(
        blockwise(ladder_term, block_rows, block_rows * lax.axis_size("vir")).astype(jnp.bfloat16),
        "vir",
        scatter_dimension=0,
        tiled=True,
    ).astype(jnp.float32)
    cycle_resid = lax.psum_scatter(
        blockwise(cycle_term, block_rows, block_rows * lax.axis_size("vir")).astype(jnp.bfloat16),
        "vir",
        scatter_dimension=0,
        tiled=True,
    ).astype(jnp.float32)
    return (ladder_resid, cycle_resid)


def solution(mesh):
    return jax.shard_map(
        on_device,
        mesh=mesh,
        in_specs=(
            P(("occ", "vir"), None),
            P(("occ", "vir"), None),
            P(),
            P("occ", None),
            P("occ", None),
            P("occ", "vir"),
            P("vir", "occ"),
        ),
        out_specs=(P(("occ", "vir"), None), P(("occ", "vir"), None)),
        check_vma=False,
    )
```

profile of v0, /device:TPU:28, one launch (start us, length us, event | category | flops | bytes accessed | tf_op | source)
XLA Modules:
  0.0 862.4 jit_solution(7057035645112783085)
XLA Ops:
  15.4 10.2 %all-to-all-start = ((s32[128,4,3]{1,2,0:T(4,128)}), s32[128,4,3]{1,2,0:T(4,128)S(1)}, u32[]{:S(2)}, u32[]{:S(2)}) async-start(s32[128,4,3]{1,2,0:T(4,128)} %copy.33), calls=%async_computation.1 | async-start | bytes 524288 | tf_op jit(solution)/shard_map/all_to_all | solution.py:82
  25.6 10.3 %scatter_custom_fusion.1 = bf16[512,9216]{1,0:T(8,128)(2,1)} fusion(s32[128]{0:T(128)S(1)} %fusion.13, bf16[128,9216]{1,0:T(8,128)(2,1)} %param.11, bf16[]{:T(256)} %constant.86.clone.1), kind=kCustom, calls=%fused_computation.34 | custom fusion | bytes 9437696 | tf_op jit(solution)/shard_map/scatter | solution.py:71
  35.9 13.9 %reshape.297 = bf16[128,4,9216]{2,1,0:T(4,128)(2,1)} reshape(bf16[512,9216]{1,0:T(8,128)(2,1)} %scatter_custom_fusion.1) | data formatting | bytes 18874368 | tf_op jit(solution)/shard_map/reshape | solution.py:76
  49.8 10.0 %all-to-all-start.1 = ((bf16[128,4,9216]{2,1,0:T(4,128)(2,1)}), bf16[128,4,9216]{2,1,0:T(4,128)(2,1)}, u32[]{:S(2)}, u32[]{:S(2)}) async-start(bf16[128,4,9216]{2,1,0:T(4,128)(2,1)} %reshape.297), calls=%async_computation.2 | async-start | bytes 18874368 | tf_op jit(solution)/shard_map/all_to_all | solution.py:75
  62.2 127.4 %all-to-all-done.1 = bf16[128,4,9216]{2,1,0:T(4,128)(2,1)} async-done(((bf16[128,4,9216]{2,1,0:T(4,128)(2,1)}), bf16[128,4,9216]{2,1,0:T(4,128)(2,1)}, u32[]{:S(2)}, u32[]{:S(2)}) %all-to-all-start.1) | async-done | bytes 9437216 | tf_op jit(solution)/shard_map/all_to_all | solution.py:75
  189.5 13.3 %reshape.298 = bf16[512,9216]{1,0:T(8,128)(2,1)} reshape(bf16[128,4,9216]{2,1,0:T(4,128)(2,1)} %all-to-all-done.1) | data formatting | bytes 18874368 | tf_op jit(solution)/shard_map/reshape | solution.py:90
  202.8 8.2 copy.35
  211.0 11.9 %reshape.299 = bf16[6,96,48,96]{3,2,1,0:T(8,128)(2,1)} reshape(bf16[576,4608]{1,0:T(8,128)(2,1)} %copy.35) | data formatting | bytes 10616832 | tf_op jit(solution)/shard_map/reshape | solution.py:97
  222.9 7.7 copy.36
  230.6 12.3 %reshape.300 = bf16[48,55296]{1,0:T(8,128)(2,1)} reshape(bf16[48,6,96,96]{3,2,1,0:T(8,128)(2,1)} %copy.36) | data formatting | bytes 10616832 | tf_op jit(solution)/shard_map/reshape | solution.py:99
  245.0 275.1 %while.25 = (s32[]{:T(128)}, bf16[8,24,9216]{2,1,0:T(8,128)(2,1)}, s32[8]{0:T(128)}, s32[192,3]{0,1:T(4,128)}, s32[16]{0:T(128)}, /*index=5*/s32[512,1]{0,1:T(1,...) while((s32[]{:T(128)}, bf16[8,24,9216]{2,1,0:T(8,128)(2,1)}, ...), condition=%wide.region_10.11_spmd.clone, body=%wide.region_8.10_spmd.clone.sunk | while | flops 1743930624 | bytes 38525264 | solution.py:13
  249.8 6.8 convolution_convert_fusion.10
  266.8 6.1 reshape.342
  284.2 6.8 convolution_convert_fusion.10
  301.2 6.1 reshape.342
  318.6 6.8 convolution_convert_fusion.10
  325.4 5.1 reshape.341
  335.5 6.1 reshape.342
  353.0 6.8 convolution_convert_fusion.10
  369.9 6.1 reshape.342
  387.4 6.8 convolution_convert_fusion.10
  404.3 6.1 reshape.342
  421.8 6.8 convolution_convert_fusion.10
  428.6 5.1 reshape.341
  438.7 6.1 reshape.342
  456.2 6.8 convolution_convert_fusion.10
  463.0 5.1 reshape.341
  473.1 6.1 reshape.342
  490.6 6.8 convolution_convert_fusion.10
  497.4 5.1 reshape.341
  507.5 6.1 reshape.342
  520.2 8.4 copy.29
  528.6 11.8 %reshape.293 = bf16[48,96,6,96]{1,0,3,2:T(8,128)(2,1)} reshape(bf16[4608,576]{0,1:T(8,128)(2,1)} %copy.29) | data formatting | bytes 10616832 | tf_op jit(solution)/shard_map/reshape | solution.py:45
  540.4 11.1 %copy.30 = bf16[48,6,96,96]{3,2,1,0:T(8,128)(2,1)} copy(bf16[48,6,96,96]{2,0,3,1:T(8,128)(2,1)} %bitcast.104) | data formatting | bytes 10616832 | tf_op jit(solution)/shard_map/transpose | solution.py:46
  551.6 12.3 %reshape.294 = bf16[48,55296]{1,0:T(8,128)(2,1)} reshape(bf16[48,6,96,96]{3,2,1,0:T(8,128)(2,1)} %copy.30) | data formatting | bytes 10616832 | tf_op jit(solution)/shard_map/reshape | solution.py:47
  566.1 245.2 %while.24 = (s32[]{:T(128)}, bf16[8,24,9216]{2,1,0:T(8,128)(2,1)}, s32[8]{0:T(128)}, s32[192,3]{0,1:T(4,128)S(1)}, bf16[48,55296]{1,0:T(8,128)(2,1)}, /*index=5*...) while((s32[]{:T(128)}, bf16[8,24,9216]{2,1,0:T(8,128)(2,1)}, ...), condition=%wide.region_1.2_spmd.clone, body=%wide.region_0.1_spmd.clone.sunk | while | flops 724628352 | bytes 31198292 | solution.py:13
  574.0 5.1 reshape.340
  584.1 6.1 reshape.339
  604.7 5.1 reshape.340
  614.7 6.1 reshape.339
  635.3 5.1 reshape.340
  645.4 6.1 reshape.339
  676.0 6.1 reshape.339
  706.6 6.1 reshape.339
  737.3 6.1 reshape.339
  767.9 6.1 reshape.339
  798.6 6.1 reshape.339
  813.3 40.6 %reduce-scatter.3.cloned.1.call-done = bf16[24,9216]{1,0:T(8,128)(2,1)} async-done(((bf16[192,9216]{1,0:T(8,128)(2,1)}), bf16[24,9216]{1,0:T(8,128)(2,1)}) %reduce-scatter.3.cloned.1.call-update) | async-done | bytes 442384 | tf_op jit(solution)/shard_map/reduce_scatter | solution.py:123
  (244 shorter events, 320.0 us)
Async XLA Ops:
  7.2 195.7 %all-gather.5.cloned.1.call-start = ((), (), s32[]{:S(2)}) async-start(), calls=%async_computation.6 | async-start | bytes 6266880 | tf_op jit(solution)/shard_map/all_gather | solution.py:95
  15.4 34.5 %all-to-all-start = ((s32[128,4,3]{1,2,0:T(4,128)}), s32[128,4,3]{1,2,0:T(4,128)S(1)}, u32[]{:S(2)}, u32[]{:S(2)}) async-start(s32[128,4,3]{1,2,0:T(4,128)} %copy.33), calls=%async_computation.1 | async-start | bytes 524288 | tf_op jit(solution)/shard_map/all_to_all | solution.py:82
  49.8 11.0 %copy-start = (s32[256]{0:T(256)S(1)}, s32[256]{0:T(256)}, u32[]{:S(2)}) copy-start(s32[256]{0:T(256)} %param.13) | copy-start | bytes 3076
  49.8 139.7 %all-to-all-start.1 = ((bf16[128,4,9216]{2,1,0:T(4,128)(2,1)}), bf16[128,4,9216]{2,1,0:T(4,128)(2,1)}, u32[]{:S(2)}, u32[]{:S(2)}) async-start(bf16[128,4,9216]{2,1,0:T(4,128)(2,1)} %reshape.297), calls=%async_computation.2 | async-start | bytes 18874368 | tf_op jit(solution)/shard_map/all_to_all | solution.py:75
  59.8 460.4 %all-gather.3.cloned.1.call-start = ((), (), s32[]{:S(2)}) async-start(), calls=%async_computation.4 | async-start | bytes 6266880 | tf_op jit(solution)/shard_map/all_gather | solution.py:43
  60.6 750.7 %reduce-scatter.5.cloned.1.call-start = ((), (), s32[]{:S(2)}) async-start(), calls=%async_computation.7 | async-start | bytes 3981312 | tf_op jit(solution)/shard_map/reduce_scatter | solution.py:129
  520.2 333.8 %reduce-scatter.3.cloned.1.call-start = ((), (), s32[]{:S(2)}) async-start(), calls=%async_computation.5 | async-start | bytes 3981312 | tf_op jit(solution)/shard_map/reduce_scatter | solution.py:123
  563.9 2.2 copy-start.1
  563.9 2.2 copy-start.2
  563.9 2.2 copy-start.3
Sparse Core Ops, SparseCore 0:
  10.2 143.2 all-gather.4
  155.7 69.4 all-gather.2
  520.3 42.4 reduce-scatter.4
  811.4 42.4 reduce-scatter.2
where the time goes:
time: 871 us; the launch traced here: 862 us
  local copies, waits for them, and re-layouts  380 us (44%)
  matrix products  227 us (26%)
  waiting for transfers between devices  169 us (19%)
  loops' own time  31.6 us (4%)
  starting transfers between devices  20.6 us (2%)
  other arithmetic  20 us (2%)
  between operations  13.9 us (2%)
    all_to_all x1, waiting for transfers between devices, on_device(): lax.all_to_all(send_tiles.reshape(device_count, capacity, tile_area), ('o...  127 us
    dot_general x16, matrix products, pick_tiles(): jnp.dot(flat, tiles, preferred_element_type=jnp.float32).astype(tiles.dtype)  86.2 us
    reshape x16, local copies, waits for them, and re-layouts, pick_tiles(): return chosen.reshape(matches.shape[0], matches.shape[1], TILE, TILE)  81.9 us
    dot_general x16, matrix products, select_rows(): jnp.dot(onehot, table, preferred_element_type=jnp.float32)  79.4 us
    reshape x8, local copies, waits for them, and re-layouts, ladder_term(): select_rows(x_table, slot_rows[:, 1])  48.8 us
    reshape x8, local copies, waits for them, and re-layouts, cycle_term(): select_rows(y_table, slot_rows[:, 2])  48.5 us
    reduce_scatter x1, waiting for transfers between devices, on_device(): lax.psum_scatter(blockwise(ladder_term, block_rows, block_rows * lax.axis...  40.6 us
    another operation x2, loops' own time, blockwise(): pieces = lax.map(lambda block_first: term(block_first, block_rows), firsts)  31.6 us
  transfers between devices with their start and end apart: 6, of which 2 were waited for; matrix products, arithmetic and copies ran while one was open for 72% of the time, Pallas kernels for 0%

commit v1 on v0

v1 whole, which is shorter than its diff:
```python
import functools

import jax
import jax.numpy as jnp
from jax import lax
from jax.experimental import pallas as pl
from jax.experimental.pallas import tpu as pltpu
from jax.sharding import PartitionSpec as P

TILE = 96
NV = 48
AREA = TILE * TILE
OCC = 16
VIR = 8
VT = 6
PAIRS = 16
VCAP = 32
BLOCKS = 288
ROWS = 192


def rows_kernel(swap, index_ref, table_ref, tiles_ref, out_ref, blocks):
    def unpack(row, carry):
        strip = table_ref[pl.ds(pl.multiple_of(row * TILE, TILE), TILE), :]
        for c in range(6):
            blocks[row * 6 + c] = strip[:, c * TILE : (c + 1) * TILE]
        return carry

    lax.fori_loop(0, NV, unpack, 0)
    blocks[BLOCKS] = jnp.zeros((TILE, TILE), blocks.dtype)

    def octet(q, carry):
        for j in range(8):
            row = q * 8 + j
            total = None
            for half in range(2):
                block = blocks[index_ref[half * ROWS + row]]
                tile = tiles_ref[index_ref[(2 + half) * ROWS + row]]
                left, right = (tile, block) if swap else (block, tile)
                part = jnp.dot(left, right, preferred_element_type=jnp.float32)
                total = part if total is None else total + part
            out_ref[q, :, j * TILE : (j + 1) * TILE] = total.astype(out_ref.dtype)
        return carry

    lax.fori_loop(0, ROWS // 8, octet, 0)


def rows_call(swap, index, table, tiles, name):
    return pl.pallas_call(
        functools.partial(rows_kernel, swap),
        out_shape=jax.ShapeDtypeStruct((ROWS // 8, TILE, 8 * TILE), jnp.bfloat16),
        in_specs=[
            pl.BlockSpec(memory_space=pltpu.SMEM),
            pl.BlockSpec(memory_space=pltpu.VMEM),
            pl.BlockSpec(memory_space=pltpu.VMEM),
        ],
        out_specs=pl.BlockSpec(memory_space=pltpu.VMEM),
        scratch_shapes=[pltpu.VMEM((BLOCKS + 1, TILE, TILE), jnp.bfloat16)],
        compiler_params=pltpu.CompilerParams(vmem_limit_bytes=48 * 1024 * 1024),
        cost_estimate=pl.CostEstimate(flops=2 * 2 * ROWS * TILE**3, bytes_accessed=14_000_000, transcendentals=0),
        name=name,
    )(index.reshape(-1), table, tiles)


def lookup(ids, table):
    flat = table.reshape(-1)
    hits = ids[..., None] == jnp.arange(flat.shape[0], dtype=jnp.int32)
    return jnp.sum(jnp.where(hits, flat, 0), axis=-1)


def before(counts, axis):
    return jnp.cumsum(counts, axis=axis) - counts


def on_device(t_tiles, t_index, cycle_map, ladder_slots, cycle_slots, x_ints, y_ints):
    occ = lax.axis_index("occ")
    vir = lax.axis_index("vir")
    i32 = jnp.int32
    local = t_index[:, 0] - occ * PAIRS
    first = t_index[:, 1] - vir * VT
    second = t_index[:, 2]

    marks = jnp.arange(PAIRS * VT, dtype=i32)[None, :] == (local * VT + first)[:, None]
    held = jnp.max(marks.astype(i32), axis=0)
    gathered = lax.all_gather(held, ("occ", "vir"), axis=0, tiled=False)
    domain = gathered.reshape(OCC, VIR, PAIRS, VT).transpose(0, 2, 1, 3)
    x_rows = lax.all_gather(x_ints, "occ", axis=0, tiled=True)
    y_pack = (
        y_ints.reshape(3, 2, TILE, 3, TILE).transpose(0, 2, 1, 3, 4).reshape(3 * TILE, 6 * TILE)
    )
    y_rows = lax.all_gather(y_pack, "occ", axis=0, tiled=True)

    def tables(dom):
        counts = jnp.sum(dom, axis=-1)
        rank_in = before(dom, 2)
        rank_all = rank_in + before(counts, 1)[..., None]
        return counts, rank_in, rank_all

    mine = lax.dynamic_index_in_dim(domain, occ, 0, keepdims=False)
    counts, rank_in, rank_all = tables(mine)
    products = counts[:, :, None] * counts[:, None, :]
    starts = before(products, 0)

    own_counts = lax.dynamic_index_in_dim(counts, vir, 1, keepdims=False)
    own_starts = lax.dynamic_index_in_dim(starts, vir, 1, keepdims=False)
    own_rank = lax.dynamic_index_in_dim(rank_in, vir, 1, keepdims=False)
    send_table = (
        jnp.arange(VIR, dtype=i32)[None, :, None] * VCAP
        + own_starts[:, :, None]
        + rank_in * own_counts[:, None, None]
    )
    which = lookup(local * VT + first, own_rank)
    position = lookup(local * NV + second, send_table) + which
    pick = jnp.arange(VIR * VCAP, dtype=i32)[:, None] == position[None, :]
    send = jnp.dot(pick.astype(jnp.bfloat16), t_tiles, preferred_element_type=jnp.float32).astype(jnp.bfloat16)
    across = lax.all_to_all(send.reshape(VIR, VCAP, AREA), "vir", split_axis=0, concat_axis=0, tiled=True)

    to_starts = lax.dynamic_index_in_dim(starts, vir, 2, keepdims=False)
    source = (jnp.arange(VIR, dtype=i32)[None, :] * VCAP + to_starts)[:, :, None] + rank_in
    source = jnp.arange(2, dtype=i32)[None, :, None, None] * counts[:, None, :, None] + source[:, None]
    at_rank = (rank_all.reshape(PAIRS, NV)[:, None, :] == jnp.arange(8, dtype=i32)[None, :, None]) & (
        mine.reshape(PAIRS, NV)[:, None, :] > 0
    )
    by_rank = jnp.sum(
        jnp.where(at_rank[:, None], source.reshape(PAIRS, 2, 1, NV), 0), axis=-1
    )
    alive = jnp.arange(2, dtype=i32)[None, :] < own_counts[:, None]
    by_rank = jnp.where(alive[:, :, None], by_rank, -1)
    own_map = lax.dynamic_slice_in_dim(cycle_map, occ * PAIRS, PAIRS, 0)
    to_group = own_map[None, :] == jnp.arange(OCC, dtype=i32)[:, None]
    by_group = jnp.sum(jnp.where(to_group[:, :, None], by_rank.reshape(1, PAIRS, 16), 0), axis=1)
    pick2 = by_group.reshape(-1)[:, None] == jnp.arange(VIR * VCAP, dtype=i32)[None, :]
    send2 = jnp.dot(
        pick2.astype(jnp.bfloat16), across.reshape(-1, AREA), preferred_element_type=jnp.float32
    ).astype(jnp.bfloat16)
    got = lax.all_to_all(send2.reshape(OCC, 16, AREA), "occ", split_axis=0, concat_axis=0, tiled=True)

    tile_key = (local * 2 + which) * NV + second
    row_key = (
        ladder_slots[:, 0][None, :] * 2 + jnp.arange(2, dtype=i32)[:, None]
    ) * NV + ladder_slots[:, 2][None, :]
    match = row_key[:, :, None] == tile_key[None, None, :]
    packed = jnp.arange(128, dtype=i32) * 8 + first + 1
    found = jnp.sum(jnp.where(match, packed, 0), axis=-1)
    ladder_tile = jnp.where(found > 0, (found - 1) // 8, 0)
    ladder_block = jnp.where(found > 0, ladder_slots[:, 1][None, :] * VT + (found - 1) % 8, BLOCKS)
    ladder_index = jnp.concatenate([ladder_block, ladder_tile], axis=0)
    ladder = rows_call(False, ladder_index, x_rows, t_tiles.reshape(128, TILE, TILE), "ladder")
    ladder_sum = lax.psum_scatter(ladder, "vir", scatter_dimension=0, tiled=True)

    owner = (cycle_map.reshape(OCC, PAIRS) == occ).astype(i32)
    owner_of = jnp.sum(owner * jnp.arange(OCC, dtype=i32)[:, None], axis=0)
    theirs = jnp.sum(owner[:, :, None, None] * domain, axis=0)
    counts_c, rank_in_c, rank_all_c = tables(theirs)
    here = lax.dynamic_index_in_dim(theirs, vir, 1, keepdims=False)
    here_rank = lax.dynamic_index_in_dim(rank_in_c, vir, 1, keepdims=False)
    ds = jnp.sum(
        jnp.where(
            (here_rank[:, None, :] == jnp.arange(2, dtype=i32)[None, :, None]) & (here[:, None, :] > 0),
            jnp.arange(1, VT + 1, dtype=i32),
            0,
        ),
        axis=-1,
    )
    s, a, b = cycle_slots[:, 0], cycle_slots[:, 1], cycle_slots[:, 2]
    rank_a = lookup(s * NV + a, rank_all_c)
    row_ds = lookup(s[None, :] * 2 + jnp.arange(2, dtype=i32)[:, None], ds)
    d = row_ds - 1
    cycle_block = ((b // 3) * 3 + d // 2) * 6 + (d % 2) * 3 + b % 3
    cycle_block = jnp.where(row_ds > 0, cycle_block, BLOCKS)
    cycle_tile = lookup(s, owner_of) * 16 + jnp.arange(2, dtype=i32)[:, None] * 8 + rank_a
    cycle_index = jnp.concatenate([cycle_block, cycle_tile], axis=0)
    cycle = rows_call(True, cycle_index, y_rows, got.reshape(256, TILE, TILE), "cycle")
    cycle_sum = lax.psum_scatter(cycle, "vir", scatter_dimension=0, tiled=True)

    def finish(octets):
        return octets.astype(jnp.float32).reshape(3, TILE, 8, TILE).transpose(0, 2, 1, 3).reshape(24, AREA)

    return finish(ladder_sum), finish(cycle_sum)


def solution(mesh):
    return jax.shard_map(
        on_device,
        mesh=mesh,
        in_specs=(
            P(("occ", "vir"), None),
            P(("occ", "vir"), None),
            P(),
            P("occ", None),
            P("occ", None),
            P("occ", "vir"),
            P("vir", "occ"),
        ),
        out_specs=(P(("occ", "vir"), None), P(("occ", "vir"), None)),
        check_vma=False,
    )
```

time: 871 us -> 376 us (0.43)
  local copies, waits for them, and re-layouts: 380 us -> 43.5 us
  matrix products: 227 us -> 9.33 us
  blocking collectives: 0 us -> 66.3 us
  Pallas kernels: 0 us -> 41.2 us
  loops' own time: 31.6 us -> 0 us
    reshape x40 -> x16, local copies, waits for them, and re-layouts: 256 us -> 25.5 us  [the longest x1 10 us: on_device(): got.reshape(256, TILE, TILE)]
    dot_general x48 -> x2, matrix products: 227 us -> 9.33 us  [the longest x1 5.86 us: on_device(): jnp.dot(pick2.astype(jnp.bfloat16), across.reshape(-1, AREA), preferred_e...]
    unnamed x0 -> x1, blocking collectives: none -> 66.3 us
    pallas_call x0 -> x2, Pallas kernels: none -> 41.2 us  [rows_call(): pl.pallas_call(functools.partial(rows_kernel, swap), out_shape=jax.ShapeD...]
    another operation x2 -> x0, loops' own time: 31.6 us -> none  [blockwise(): pieces = lax.map(lambda block_first: term(block_first, block_rows), firsts)]
    broadcast_in_dim x16 -> x0, local copies, waits for them, and re-layouts: 30.4 us -> none  [blockwise(): pieces = lax.map(lambda block_first: term(block_first, block_rows), firsts)]
    dynamic_slice x32 -> x7, local copies, waits for them, and re-layouts: 25.6 us -> 2.9 us  [the longest x2 0.77 us: on_device(): mine = lax.dynamic_index_in_dim(domain, occ, 0, keepdims=False)]
    transpose x2 -> x0, local copies, waits for them, and re-layouts: 18.8 us -> none  [the longest x1 11.1 us: on_device(): x_table = x_rows.reshape(NV, TILE, vir_tiles, TILE).transpose(0, 2, 1, 3)...]
  transfers between devices with their start and end apart: 6 -> 6, of which waited for: 2 -> 4; matrix products, arithmetic and copies ran while one was open for 72% -> 17% of each run, Pallas kernels for 0% -> 11%
where the time goes in v1:
time: 376 us; the launch traced here: 374 us
  waiting for transfers between devices  168 us (45%)
  blocking collectives  66.3 us (18%)
  local copies, waits for them, and re-layouts  43.5 us (12%)
  Pallas kernels  41.2 us (11%)
  other arithmetic  17.9 us (5%)
  between operations  14.2 us (4%)
  starting transfers between devices  13.2 us (4%)
  matrix products  9.33 us (2%)
    all_to_all x1, waiting for transfers between devices, on_device(): lax.all_to_all(send2.reshape(OCC, 16, AREA), 'occ', split_axis=0, concat_...  72.3 us
    unnamed x1, blocking collectives  66.3 us
    all_to_all x1, waiting for transfers between devices, on_device(): lax.all_to_all(send.reshape(VIR, VCAP, AREA), 'vir', split_axis=0, concat...  49.2 us
    pallas_call x2, Pallas kernels, rows_call(): pl.pallas_call(functools.partial(rows_kernel, swap), out_shape=jax.ShapeD...  41.2 us
    reduce_scatter x1, waiting for transfers between devices, on_device(): lax.psum_scatter(ladder, 'vir', scatter_dimension=0, tiled=True)  34.4 us
    reduce_scatter x1, waiting for transfers between devices, on_device(): cycle_sum = lax.psum_scatter(cycle, 'vir', scatter_dimension=0, tiled=True)  11.5 us
    reshape x1, local copies, waits for them, and re-layouts, on_device(): got.reshape(256, TILE, TILE)  10 us
    all_to_all x1, starting transfers between devices, on_device(): lax.all_to_all(send2.reshape(OCC, 16, AREA), 'occ', split_axis=0, concat_...  8.11 us
  transfers between devices with their start and end apart: 6, of which 4 were waited for; matrix products, arithmetic and copies ran while one was open for 17% of the time, Pallas kernels for 11%

profile of v1, /device:TPU:28, one launch (start us, length us, event | category | flops | bytes accessed | tf_op | source)
XLA Modules:
  0.0 373.9 jit_solution(9135530433025631441)
XLA Ops:
  7.2 1.8 reshape.413
  9.0 0.9 copy.96
  9.9 1.1 reshape.414
  11.1 0.7 all-gather.4.cloned.1.call-update
  11.8 1.3 add_bitcast_fusion.1
  13.8 66.3 %all-reduce = s32[12288]{0:T(1024)S(1)} all-reduce(s32[12288]{0:T(1024)S(1)} %dynamic-update-slice), channel_id=2, replica_groups=mesh['occ'=16,'vir'=8] {'occ','vir'}, use_global_device_ids=true, to_apply=%add | all-reduce | flops 12288 | bytes 98304
  80.1 1.0 reshape.404
  81.4 0.6 dynamic-slice_bitcast_fusion
  82.7 0.8 copy.101
  84.1 0.9 copy.102
  85.7 3.6 reduce_window_sum.49
  89.8 0.8 constant_dynamic-slice_fusion.2
  90.7 0.7 add.342
  91.4 1.0 add.343
  92.4 1.3 mul.244
  93.7 1.0 mul.245
  95.3 1.0 reduce_window_sum.55
  96.3 0.7 copy.108
  96.9 1.6 squeeze.29
  98.5 1.3 multiply_add_fusion
  99.8 0.7 dynamic-slice_subtract_fusion
  100.6 0.7 select_reduce_fusion.6
  101.3 0.9 select_reduce_fusion.1
  102.1 1.3 bitcast_add_fusion.2
  103.5 3.5 convolution_convert_fusion
  106.9 4.7 %all-to-all-start = ((bf16[8,32,9216]{2,1,0:T(8,128)(2,1)}), bf16[8,32,9216]{2,1,0:T(8,128)(2,1)}, u32[]{:S(2)}, u32[]{:S(2)}) async-start(bf16[8,32,9216]{2,1,0:T(8,128)(2,1)} %bitcast.73), calls=%async_computation.1 | async-start | bytes 9437184 | tf_op jit(solution)/shard_map/all_to_all | solution.py:116
  111.7 0.7 copy.97
  112.6 0.8 add_bitcast_fusion
  113.4 0.8 reduce_window_sum.52
  114.9 0.8 bitcast_add_fusion
  115.8 0.6 select_reduce_fusion.4
  116.8 0.8 dynamic_slice.32
  117.7 49.2 %all-to-all-done = bf16[8,32,9216]{2,1,0:T(8,128)(2,1)} async-done(((bf16[8,32,9216]{2,1,0:T(8,128)(2,1)}), bf16[8,32,9216]{2,1,0:T(8,128)(2,1)}, u32[]{:S(2)}, u32[]{:S(2)}) %all-to-all-start) | async-done | bytes 4718624 | tf_op jit(solution)/shard_map/all_to_all | solution.py:116
  167.0 5.9 %convolution_convert_fusion.1 = bf16[256,9216]{1,0:T(8,128)(2,1)} fusion(bf16[256,9216]{1,0:T(8,128)(2,1)} %bitcast.27, s32[256]{0:T(256)S(1)} %eq.219), kind=kOutput, calls=%fused_computation.1 | convolution fusion | flops 1210384384 | bytes 9438208 | tf_op jit(solution)/shard_map/dot_general | solution.py:133
  172.9 8.1 %all-to-all-start.1 = ((bf16[16,16,9216]{2,1,0:T(8,128)(2,1)}), bf16[16,16,9216]{2,1,0:T(8,128)(2,1)}, u32[]{:S(2)}, u32[]{:S(2)}) async-start(bf16[16,16,9216]{2,1,0:T(8,128)(2,1)} %bitcast.72), calls=%async_computation.2 | async-start | bytes 9437184 | tf_op jit(solution)/shard_map/all_to_all | solution.py:136
  181.5 1.3 reduce_window_sum.50
  184.6 72.3 %all-to-all-done.1 = bf16[16,16,9216]{2,1,0:T(8,128)(2,1)} async-done(((bf16[16,16,9216]{2,1,0:T(8,128)(2,1)}), bf16[16,16,9216]{2,1,0:T(8,128)(2,1)}, u32[]{:S(2)}, u32[]{:S(2)}) %all-to-all-start.1) | async-done | bytes 4718624 | tf_op jit(solution)/shard_map/all_to_all | solution.py:136
  256.9 10.0 %reshape.418.tiles_ref = bf16[256,96,96]{2,1,0:T(8,128)(2,1)} reshape(bf16[16,16,9216]{2,1,0:T(8,128)(2,1)} %all-to-all-done.1) | data formatting | bytes 9437184 | tf_op jit(solution)/shard_map/reshape | solution.py:173
  266.9 21.5 %cycle.1 = bf16[24,96,768]{2,1,0:T(8,128)(2,1)} custom-call(s32[768]{0:T(1024)S(1)} %reshape.412.index_ref, bf16[4608,576]{1,0:T(8,128)(2,1)} %all-gather.6.cloned.1.call-done.table_ref, bf16[256,96,96]{2,1,0:T(8,128)(2,1)} %reshape.418.tiles_ref), custom_call_target="tpu_custom_call" | custom-call | flops 679477248 | bytes 14000000 | tf_op jit(solution)/shard_map/cycle/pallas_call | solution.py:49
  288.7 2.5 copy.89
  291.3 3.5 copy.90.tiles_ref
  294.9 19.7 %ladder.1 = bf16[24,96,768]{2,1,0:T(8,128)(2,1)} custom-call(s32[768]{0:T(1024)S(1)} %reshape.406.index_ref, bf16[4608,576]{1,0:T(8,128)(2,1)} %all-gather.4.cloned.1.call-done.table_ref, bf16[128,96,96]{2,1,0:T(8,128)(2,1)S(1)} %copy.90.tiles_ref), custom_call_target="tpu_custom_call" | custom-call | flops 679477248 | bytes 14000000 | tf_op jit(solution)/shard_map/ladder/pallas_call | solution.py:49
  314.6 11.5 %reduce-scatter.5.cloned.1.call-done = bf16[3,96,768]{2,1,0:T(8,128)(2,1)} async-done(((bf16[24,96,768]{2,1,0:T(8,128)(2,1)}), bf16[3,96,768]{2,1,0:T(8,128)(2,1)}) %reduce-scatter.5.cloned.1.call-update) | async-done | bytes 442384 | tf_op jit(solution)/shard_map/reduce_scatter | solution.py:174
  326.2 1.6 reshape.431
  327.9 1.6 reshape.425
  329.6 34.4 %reduce-scatter.3.cloned.1.call-done = bf16[3,96,768]{2,1,0:T(8,128)(2,1)} async-done(((bf16[24,96,768]{2,1,0:T(8,128)(2,1)}), bf16[3,96,768]{2,1,0:T(8,128)(2,1)}) %reduce-scatter.3.cloned.1.call-update) | async-done | bytes 442384 | tf_op jit(solution)/shard_map/reduce_scatter | solution.py:149
  364.0 1.6 reshape.429
  365.8 1.6 reshape.423
  (103 shorter events, 8.8 us)
Async XLA Ops:
  7.2 96.3 %copy-start = (bf16[128,9216]{1,0:T(8,128)(2,1)S(1)}, bf16[128,9216]{1,0:T(8,128)(2,1)}, u32[]{:S(2)}) copy-start(bf16[128,9216]{1,0:T(8,128)(2,1)} %param.7) | copy-start | bytes 7077892
  7.2 259.8 %all-gather.6.cloned.1.call-start = ((), (), s32[]{:S(2)}) async-start(), calls=%async_computation.6 | async-start | bytes 6266880 | tf_op jit(solution)/shard_map/all_gather | solution.py:91
  11.0 283.8 %all-gather.4.cloned.1.call-start = ((), (), s32[]{:S(2)}) async-start(), calls=%async_computation.4 | async-start | bytes 6266880 | tf_op jit(solution)/shard_map/all_gather | solution.py:87
  11.8 78.8 %copy-start.6 = (s32[8]{0:T(128)}, s32[8]{0:T(128)S(1)}, u32[]{:S(2)}) copy-start(s32[8]{0:T(128)S(1)} %iota_multiply_fusion.1) | copy-start | bytes 100
  13.1 0.5 copy-start.9
  106.9 5.6 %copy-start.7 = (s32[8]{0:T(128)S(1)}, s32[8]{0:T(128)}, u32[]{:S(2)}) copy-start(s32[8]{0:T(128)} %copy-done.6) | copy-start | bytes 100
  106.9 9.5 %copy-start.3 = (s32[16]{0:T(128)S(1)}, s32[16]{0:T(128)}, u32[]{:S(2)}) copy-start(s32[16]{0:T(128)} %fusion.11) | copy-start | bytes 196
  106.9 60.0 %all-to-all-start = ((bf16[8,32,9216]{2,1,0:T(8,128)(2,1)}), bf16[8,32,9216]{2,1,0:T(8,128)(2,1)}, u32[]{:S(2)}, u32[]{:S(2)}) async-start(bf16[8,32,9216]{2,1,0:T(8,128)(2,1)} %bitcast.73), calls=%async_computation.1 | async-start | bytes 9437184 | tf_op jit(solution)/shard_map/all_to_all | solution.py:116
  172.8 8.2 %copy-start.8 = (s32[256]{0:T(256)S(1)}, s32[256]{0:T(256)}, u32[]{:S(2)}) copy-start(s32[256]{0:T(256)} %param.9) | copy-start | bytes 3076
  172.8 10.8 %copy-start.1 = (s32[192,3]{0,1:T(4,128)S(1)}, s32[192,3]{0,1:T(4,128)}, u32[]{:S(2)}) copy-start(s32[192,3]{0,1:T(4,128)} %param.11) | copy-start | bytes 6916
  172.8 11.0 %copy-start.2 = (s32[192,3]{0,1:T(4,128)S(1)}, s32[192,3]{0,1:T(4,128)}, u32[]{:S(2)}) copy-start(s32[192,3]{0,1:T(4,128)} %param.10) | copy-start | bytes 6916
  172.8 11.0 %copy-start.4 = (s32[128]{0:T(128)S(1)}, s32[128]{0:T(128)}, u32[]{:S(2)}) copy-start(s32[128]{0:T(128)} %get-tuple-element.21) | copy-start | bytes 1540
  172.8 11.0 %copy-start.5 = (s32[128]{0:T(128)S(1)}, s32[128]{0:T(128)}, u32[]{:S(2)}) copy-start(s32[128]{0:T(128)} %get-tuple-element.22) | copy-start | bytes 1540
  172.9 84.1 %all-to-all-start.1 = ((bf16[16,16,9216]{2,1,0:T(8,128)(2,1)}), bf16[16,16,9216]{2,1,0:T(8,128)(2,1)}, u32[]{:S(2)}, u32[]{:S(2)}) async-start(bf16[16,16,9216]{2,1,0:T(8,128)(2,1)} %bitcast.72), calls=%async_computation.2 | async-start | bytes 9437184 | tf_op jit(solution)/shard_map/all_to_all | solution.py:136
  181.0 145.2 %reduce-scatter.5.cloned.1.call-start = ((), (), s32[]{:S(2)}) async-start(), calls=%async_computation.7 | async-start | bytes 3981312 | tf_op jit(solution)/shard_map/reduce_scatter | solution.py:174
  288.5 75.5 %reduce-scatter.3.cloned.1.call-start = ((), (), s32[]{:S(2)}) async-start(), calls=%async_computation.5 | async-start | bytes 3981312 | tf_op jit(solution)/shard_map/reduce_scatter | solution.py:149
Sparse Core Ops, SparseCore 0:
  11.2 60.1 all-gather.5
  73.5 59.2 all-gather.3
  288.6 37.5 reduce-scatter.4
  328.6 35.3 reduce-scatter.2

commit v2 on v1

v2 whole, which is shorter than its diff:
```python
import functools

import jax
import jax.numpy as jnp
from jax import lax
from jax.experimental import pallas as pl
from jax.experimental.pallas import tpu as pltpu
from jax.sharding import PartitionSpec as P

TILE = 96
NV = 48
AREA = TILE * TILE
OCC = 16
VIR = 8
VT = 6
PAIRS = 16
VCAP = 32
BLOCKS = 288
ROWS = 192
WIDE = 8 * TILE
H = 2
R = TILE // H
HALF = 144
MESH = pl.DeviceIdType.MESH
VPACK, OPACK, LADDER, CYCLE = 0, 256, 512, 512 + 4 * ROWS


def marks_kernel(mark_ref, out_ref, got, rows, table, send1, recv1, send2, recv2):
    occ, vir = lax.axis_index("occ"), lax.axis_index("vir")
    barrier = pltpu.get_barrier_semaphore()
    for k in range(1, VIR):
        pl.semaphore_signal(barrier, inc=1, device_id=(occ, (vir + k) % VIR), device_id_type=MESH)
    for k in range(1, OCC):
        pl.semaphore_signal(barrier, inc=1, device_id=((occ + k) % OCC, vir), device_id_type=MESH)
    pl.semaphore_wait(barrier, VIR + OCC - 2)
    copies = []
    for k in range(1, VIR):
        copy = pltpu.make_async_remote_copy(
            mark_ref, got.at[k - 1], send1.at[k - 1], recv1.at[k - 1],
            device_id=(occ, (vir + VIR - k) % VIR), device_id_type=MESH,
        )
        copy.start()
        copies.append(copy)
    line = lax.broadcasted_iota(jnp.int32, (8, 128), 0)
    all_rows = jnp.where(line == vir, mark_ref[...], 0)
    for k in range(1, VIR):
        copies[k - 1].wait_recv()
        all_rows = jnp.where(line == (vir + k) % VIR, got[k - 1], all_rows)
    rows[...] = all_rows
    for k in range(1, OCC):
        copy = pltpu.make_async_remote_copy(
            rows, table.at[k - 1], send2.at[k - 1], recv2.at[k - 1],
            device_id=((occ + OCC - k) % OCC, vir), device_id_type=MESH,
        )
        copy.start()
        copies.append(copy)
    out_ref[0] = all_rows
    for k in range(1, OCC):
        copies[VIR - 2 + k].wait_recv()
        out_ref[k] = table[k - 1]
    for copy in copies:
        copy.wait_send()


def marks_call(mark):
    return pl.pallas_call(
        marks_kernel,
        out_shape=jax.ShapeDtypeStruct((OCC, 8, 128), jnp.int32),
        in_specs=[pl.BlockSpec(memory_space=pltpu.VMEM)],
        out_specs=pl.BlockSpec(memory_space=pltpu.VMEM),
        scratch_shapes=[
            pltpu.VMEM((VIR - 1, 8, 128), jnp.int32),
            pltpu.VMEM((8, 128), jnp.int32),
            pltpu.VMEM((OCC - 1, 8, 128), jnp.int32),
            pltpu.SemaphoreType.DMA((VIR - 1,)),
            pltpu.SemaphoreType.DMA((VIR - 1,)),
            pltpu.SemaphoreType.DMA((OCC - 1,)),
            pltpu.SemaphoreType.DMA((OCC - 1,)),
        ],
        compiler_params=pltpu.CompilerParams(collective_id=0, has_side_effects=True),
        name="marks",
    )(mark)


def main_kernel(
    index_ref, t_ref, x_ref, y_ref, ladder_ref, cycle_ref,
    x_got, y_got, blocks, v_send, v_got, v_tiles, o_send, o_got, o_tiles,
    l_part, l_core, l_z, c_part, c_core, c_z,
    g_ss, g_rs, v_ss, v_rs, o_ss, o_rs, core_ss, core_rs, z_ss, z_rs,
):
    occ, vir = lax.axis_index("occ"), lax.axis_index("vir")
    ox, oy = occ // 4, occ % 4
    z, core = vir // 2, vir % 2
    barrier = pltpu.get_barrier_semaphore()
    for k in range(1, VIR):
        pl.semaphore_signal(barrier, inc=1, device_id=(occ, (vir + k) % VIR), device_id_type=MESH)
    for k in range(1, OCC):
        pl.semaphore_signal(barrier, inc=1, device_id=((occ + k) % OCC, vir), device_id_type=MESH)

    def v_pack(q, carry):
        for j in range(8):
            tile = t_ref[index_ref[VPACK + q * 8 + j]]
            for h in range(H):
                v_send[h, q // 4, q % 4, :, j * TILE : (j + 1) * TILE] = tile[h * R : (h + 1) * R]
        return carry

    lax.fori_loop(0, VIR * 4, v_pack, 0)
    pl.semaphore_wait(barrier, VIR + OCC - 2)
    sent = []

    def push(src, dst, ssem, rsem, device):
        copy = pltpu.make_async_remote_copy(src, dst, ssem, rsem, device_id=device, device_id_type=MESH)
        copy.start()
        sent.append(copy)
        return copy

    def v_push(h):
        return [
            push(v_send.at[h, k], v_got.at[h, VIR - k - 1], v_ss.at[h, k - 1], v_rs.at[h, VIR - k - 1],
                 (occ, (vir + k) % VIR))
            for k in range(1, VIR)
        ]

    shards = (x_ref, y_ref)
    landing = (x_got, y_got)

    def place(array, half, rel):
        rows = pl.ds(half * HALF, HALF)
        return shards[array].at[rows] if rel == 0 else landing[array].at[rel - 1, rows]

    def spread(array, half, along_y, rel, slot):
        copies = []
        dx, dy = rel // 4, rel % 4
        for k in (1, 3, 2):
            if along_y:
                target, there = (ox * 4 + (oy + k) % 4, vir), dx * 4 + (dy + 4 - k) % 4
            else:
                target, there = (((ox + k) % 4) * 4 + oy, vir), ((dx + 4 - k) % 4) * 4 + dy
            copies.append(push(
                place(array, half, rel), landing[array].at[there - 1, pl.ds(half * HALF, HALF)],
                g_ss.at[array, half, slot * 3 + k - 1], g_rs.at[array, half, there - 1], target,
            ))
        return copies

    stage1 = {}
    stage2 = {}

    def gather_start(array):
        for half in range(2):
            stage1[array, half] = spread(array, half, half == 0, 0, 0)
            stage2[array, half] = spread(array, half, half == 1, 0, 1)

    def gather_forward(array):
        for i, k in enumerate((1, 3, 2)):
            for half in range(2):
                stage1[array, half][i].wait_recv()
                rel = 4 - k if half == 0 else (4 - k) * 4
                stage2[array, half] = stage2[array, half] + spread(array, half, half == 1, rel, 1 + k)

    def gather_unpack(array):
        for half in range(2):
            for copy in stage2[array, half]:
                copy.wait_recv()

        def unpack_from(ref, base, n):
            for row in range(3):
                strip = ref[row * TILE : (row + 1) * TILE]
                for c in range(6):
                    blocks[base + row * 6 + c] = strip[:, c * TILE : (c + 1) * TILE]

        unpack_from(shards[array], 0, 3)

        def body(n, carry):
            unpack_from(landing[array].at[n], (n + 1) * 18, 3)
            return carry

        lax.fori_loop(0, OCC - 1, body, 0)

    gather_start(0)
    v_copies = [v_push(h) for h in range(H)]
    gather_start(1)
    blocks[BLOCKS] = jnp.zeros((TILE, TILE), jnp.bfloat16)
    gather_forward(0)
    gather_forward(1)

    def split(dst, strip, base):
        for j in range(8):
            dst[base + j] = strip[:, j * TILE : (j + 1) * TILE]

    def o_step(h):
        for copy in v_copies[h]:
            copy.wait_recv()
        for q in range(4):
            split(v_tiles, v_send[h, 0, q], q * 8)

        def unpack(q, carry):
            split(v_tiles, v_got[h, q // 4, q % 4], (q + 4) * 8)
            return carry

        lax.fori_loop(0, (VIR - 1) * 4, unpack, 0)

        def pack(q, carry):
            for j in range(8):
                o_send[h, q // 2, q % 2, :, j * TILE : (j + 1) * TILE] = v_tiles[index_ref[OPACK + q * 8 + j]]
            return carry

        lax.fori_loop(0, OCC * 2, pack, 0)
        return [
            push(o_send.at[h, k], o_got.at[h, OCC - k - 1], o_ss.at[h, k - 1], o_rs.at[h, OCC - k - 1],
                 ((occ + k) % OCC, vir))
            for k in range(1, OCC)
        ]

    def products(base, tiles, part, swap):
        def octet(q, carry):
            owner = q // 3
            for j in range(8):
                row = q * 8 + j
                total = None
                for half in range(2):
                    block = blocks[index_ref[base + half * ROWS + row]]
                    tile = tiles[index_ref[base + (2 + half) * ROWS + row]]
                    left, right = (tile, block) if swap else (block, tile)
                    term = jnp.dot(left, right, preferred_element_type=jnp.float32)
                    total = term if total is None else total + term
                part[owner % 2, owner // 2, q % 3, :, j * TILE : (j + 1) * TILE] = total.astype(jnp.bfloat16)
            return carry

        lax.fori_loop(0, ROWS // 8, octet, 0)

    def core_push(n, part, dst):
        return push(part.at[1 - core], dst, core_ss.at[n], core_rs.at[n], (occ, z * 2 + 1 - core))

    def z_push(n, copy, part, dst, z_got):
        copy.wait_recv()

        def add(q, carry):
            total = part[core, q // 3, q % 3].astype(jnp.float32) + dst[q // 3, q % 3].astype(jnp.float32)
            dst[q // 3, q % 3] = total.astype(jnp.bfloat16)
            return carry

        lax.fori_loop(0, 12, add, 0)
        return [
            push(dst.at[(z + k) % 4], z_got.at[4 - k - 1], z_ss.at[n, k - 1], z_rs.at[n, 4 - k - 1],
                 (occ, ((z + k) % 4) * 2 + core))
            for k in (1, 3, 2)
        ]

    def finish(copies, dst, z_got, out, first, rows):
        for copy in copies:
            copy.wait_recv()
        for i in range(3):
            total = dst[z, i].astype(jnp.float32)
            for k in range(3):
                total = total + z_got[k, i].astype(jnp.float32)
            out[i, first : first + rows] = total

    o_copies = [o_step(h) for h in range(H)]
    gather_unpack(0)
    products(LADDER, t_ref, l_part, False)
    l_copy = core_push(H, l_part, l_core)
    gather_unpack(1)
    l_copies = z_push(H, l_copy, l_part, l_core, l_z)
    c_copies = []
    for h in range(H):
        for copy in o_copies[h]:
            copy.wait_recv()
        for j in range(2):
            split(o_tiles, o_send[h, 0, j], j * 8)

        def unpack(q, carry):
            split(o_tiles, o_got[h, q // 2, q % 2], (q + 2) * 8)
            return carry

        lax.fori_loop(0, (OCC - 1) * 2, unpack, 0)
        products(CYCLE, o_tiles, c_part.at[h], True)
        c_copies.append(core_push(h, c_part.at[h], c_core.at[h]))
        if h > 0:
            c_copies[h - 1] = z_push(h - 1, c_copies[h - 1], c_part.at[h - 1], c_core.at[h - 1], c_z.at[h - 1])
    c_copies[H - 1] = z_push(H - 1, c_copies[H - 1], c_part.at[H - 1], c_core.at[H - 1], c_z.at[H - 1])
    finish(l_copies, l_core, l_z, ladder_ref, 0, TILE)
    for h in range(H):
        finish(c_copies[h], c_core.at[h], c_z.at[h], cycle_ref, h * R, R)
    for copy in sent:
        copy.wait_send()


def main_call(index, tiles, x, y):
    bf16 = jnp.bfloat16
    vmem = pl.BlockSpec(memory_space=pltpu.VMEM)
    dma = pltpu.SemaphoreType.DMA
    out = jax.ShapeDtypeStruct((3, TILE, WIDE), jnp.float32)
    return pl.pallas_call(
        main_kernel,
        out_shape=(out, out),
        in_specs=[pl.BlockSpec(memory_space=pltpu.SMEM), vmem, vmem, vmem],
        out_specs=(vmem, vmem),
        scratch_shapes=[
            pltpu.VMEM((OCC - 1, 3 * TILE, 6 * TILE), bf16),
            pltpu.VMEM((OCC - 1, 3 * TILE, 6 * TILE), bf16),
            pltpu.VMEM((BLOCKS + 1, TILE, TILE), bf16),
            pltpu.VMEM((H, VIR, 4, R, WIDE), bf16),
            pltpu.VMEM((H, VIR - 1, 4, R, WIDE), bf16),
            pltpu.VMEM((256, R, TILE), bf16),
            pltpu.VMEM((H, OCC, 2, R, WIDE), bf16),
            pltpu.VMEM((H, OCC - 1, 2, R, WIDE), bf16),
            pltpu.VMEM((256, R, TILE), bf16),
            pltpu.VMEM((2, 4, 3, TILE, WIDE), bf16),
            pltpu.VMEM((4, 3, TILE, WIDE), bf16),
            pltpu.VMEM((3, 3, TILE, WIDE), bf16),
            pltpu.VMEM((H, 2, 4, 3, R, WIDE), bf16),
            pltpu.VMEM((H, 4, 3, R, WIDE), bf16),
            pltpu.VMEM((H, 3, 3, R, WIDE), bf16),
            dma((2, 2, 15)), dma((2, 2, 15)),
            dma((H, VIR - 1)), dma((H, VIR - 1)),
            dma((H, OCC - 1)), dma((H, OCC - 1)),
            dma((H + 1,)), dma((H + 1,)),
            dma((H + 1, 3)), dma((H + 1, 3)),
        ],
        compiler_params=pltpu.CompilerParams(
            collective_id=1, has_side_effects=True, vmem_limit_bytes=63_000_000
        ),
        cost_estimate=pl.CostEstimate(flops=8 * ROWS * TILE**3, bytes_accessed=14_000_000, transcendentals=0),
        name="contract",
    )(index, tiles, x, y)


def lookup(ids, table):
    flat = table.reshape(-1)
    hits = ids[..., None] == jnp.arange(flat.shape[0], dtype=jnp.int32)
    return jnp.sum(jnp.where(hits, flat, 0), axis=-1)


def before(counts, axis):
    return jnp.cumsum(counts, axis=axis) - counts


def on_device(t_tiles, t_index, cycle_map, ladder_slots, cycle_slots, x_ints, y_ints):
    occ = lax.axis_index("occ")
    vir = lax.axis_index("vir")
    i32 = jnp.int32
    local = t_index[:, 0] - occ * PAIRS
    first = t_index[:, 1] - vir * VT
    second = t_index[:, 2]
    pair_range = jnp.arange(2, dtype=i32)
    vir_range = jnp.arange(VIR, dtype=i32)

    marks = jnp.arange(128, dtype=i32)[None, :] == (local * VT + first)[:, None]
    held = jnp.max(marks.astype(i32), axis=0)
    table = marks_call(jnp.broadcast_to(held[None], (8, 128)))
    domain = table[:, :, : PAIRS * VT].reshape(OCC, VIR, PAIRS, VT).transpose(0, 2, 1, 3)

    def tables(dom):
        counts = jnp.sum(dom, axis=-1)
        rank_in = before(dom, 2)
        rank_all = rank_in + before(counts, 1)[..., None]
        return counts, rank_in, rank_all

    mine = domain[0]
    counts, rank_in, rank_all = tables(mine)
    starts = before(counts[:, :, None] * counts[:, None, :], 0)

    own_counts = lax.dynamic_index_in_dim(counts, vir, 1, keepdims=False)
    own_starts = lax.dynamic_index_in_dim(starts, vir, 1, keepdims=False)
    own_rank = lax.dynamic_index_in_dim(rank_in, vir, 1, keepdims=False)
    send_table = (
        ((vir_range - vir) % VIR)[None, :, None] * VCAP
        + own_starts[:, :, None]
        + rank_in * own_counts[:, None, None]
    )
    which = lookup(local * VT + first, own_rank)
    position = lookup(local * NV + second, send_table) + which
    pick = jnp.arange(VIR * VCAP, dtype=i32)[:, None] == position[None, :]
    v_pack = jnp.sum(jnp.where(pick, jnp.arange(128, dtype=i32), 0), axis=1)

    to_starts = lax.dynamic_index_in_dim(starts, vir, 2, keepdims=False)
    source = (((vir_range - vir) % VIR)[None, :] * VCAP + to_starts)[:, :, None] + rank_in
    source = pair_range[None, :, None, None] * counts[:, None, :, None] + source[:, None]
    at_rank = (rank_all.reshape(PAIRS, NV)[:, None, :] == jnp.arange(8, dtype=i32)[None, :, None]) & (
        mine.reshape(PAIRS, NV)[:, None, :] > 0
    )
    by_rank = jnp.sum(jnp.where(at_rank[:, None], source.reshape(PAIRS, 2, 1, NV), 0), axis=-1)
    alive = pair_range[None, :] < own_counts[:, None]
    by_rank = jnp.where(alive[:, :, None], by_rank, 0)
    own_map = lax.dynamic_slice_in_dim(cycle_map, occ * PAIRS, PAIRS, 0)
    to_group = own_map[None, :] == ((occ + jnp.arange(OCC, dtype=i32)) % OCC)[:, None]
    o_pack = jnp.sum(jnp.where(to_group[:, :, None], by_rank.reshape(1, PAIRS, 16), 0), axis=1)

    def ahead(group):
        return ((group // 4 - occ // 4) % 4) * 4 + (group % 4 - occ % 4) % 4

    tile_key = (local * 2 + which) * NV + second
    row_key = (ladder_slots[:, 0][None, :] * 2 + pair_range[:, None]) * NV + ladder_slots[:, 2][None, :]
    match = row_key[:, :, None] == tile_key[None, None, :]
    packed = jnp.arange(128, dtype=i32) * 8 + first + 1
    found = jnp.sum(jnp.where(match, packed, 0), axis=-1)
    ladder_tile = jnp.where(found > 0, (found - 1) // 8, 0)
    x_row = ladder_slots[:, 1]
    x_block = (ahead(x_row // 3) * 3 + x_row % 3) * VT
    ladder_block = jnp.where(found > 0, x_block[None, :] + (found - 1) % 8, BLOCKS)

    by_o = (cycle_map.reshape(OCC, PAIRS) == occ).astype(i32)
    ahead_of = jnp.sum(by_o * ((jnp.arange(OCC, dtype=i32) - occ) % OCC)[:, None], axis=0)
    owner = (jnp.arange(OCC, dtype=i32)[:, None] == ahead_of[None, :]).astype(i32)
    theirs = jnp.sum(owner[:, :, None, None] * domain, axis=0)
    _, rank_in_c, rank_all_c = tables(theirs)
    here = lax.dynamic_index_in_dim(theirs, vir, 1, keepdims=False)
    here_rank = lax.dynamic_index_in_dim(rank_in_c, vir, 1, keepdims=False)
    ds = jnp.sum(
        jnp.where(
            (here_rank[:, None, :] == pair_range[None, :, None]) & (here[:, None, :] > 0),
            jnp.arange(1, VT + 1, dtype=i32),
            0,
        ),
        axis=-1,
    )
    s, a, b = cycle_slots[:, 0], cycle_slots[:, 1], cycle_slots[:, 2]
    rank_a = lookup(s * NV + a, rank_all_c)
    row_ds = lookup(s[None, :] * 2 + pair_range[:, None], ds)
    d = row_ds - 1
    cycle_block = (ahead(b // 3) * 3 + d // 2) * 6 + (d % 2) * 3 + b % 3
    cycle_block = jnp.where(row_ds > 0, cycle_block, BLOCKS)
    cycle_tile = lookup(s, ahead_of) * 16 + pair_range[:, None] * 8 + rank_a
    index = jnp.concatenate(
        [v_pack, o_pack.reshape(-1)]
        + [rows.reshape(-1) for rows in (ladder_block, ladder_tile, cycle_block, cycle_tile)]
    )
    y_pack = y_ints.reshape(3, 2, TILE, 3, TILE).transpose(0, 2, 1, 3, 4).reshape(3 * TILE, 6 * TILE)
    ladder, cycle = main_call(index, t_tiles.reshape(128, TILE, TILE), x_ints, y_pack)

    def finish(octets):
        return octets.reshape(3, TILE, 8, TILE).transpose(0, 2, 1, 3).reshape(24, AREA)

    return finish(ladder), finish(cycle)


def solution(mesh):
    return jax.shard_map(
        on_device,
        mesh=mesh,
        in_specs=(
            P(("occ", "vir"), None),
            P(("occ", "vir"), None),
            P(),
            P("occ", None),
            P("occ", None),
            P("occ", "vir"),
            P("vir", "occ"),
        ),
        out_specs=(P(("occ", "vir"), None), P(("occ", "vir"), None)),
        check_vma=False,
    )
```

time: 376 us -> 241 us (0.64)
  waiting for transfers between devices: 168 us -> 0 us
  Pallas kernels: 41.2 us -> 209 us
  blocking collectives: 66.3 us -> 0 us
  local copies, waits for them, and re-layouts: 43.5 us -> 21.9 us
  starting transfers between devices: 13.2 us -> 0 us
  between operations: 14.2 us -> 1.16 us
  other arithmetic: 17.9 us -> 8.27 us
  matrix products: 9.33 us -> 0 us
    pallas_call x2, Pallas kernels: 41.2 us -> 209 us  [the longest x1 194 us: main_call(): pl.pallas_call(main_kernel, out_shape=(out, out), in_specs=[pl.BlockSpec(...]
    all_to_all x2 -> x0, waiting for transfers between devices: 122 us -> none  [the longest x1 72.3 us: on_device(): lax.all_to_all(send2.reshape(OCC, 16, AREA), 'occ', split_axis=0, concat_...]
    unnamed x1 -> x0, blocking collectives: 66.3 us -> none
    reduce_scatter x2 -> x0, waiting for transfers between devices: 45.9 us -> none  [the longest x1 34.4 us: on_device(): lax.psum_scatter(ladder, 'vir', scatter_dimension=0, tiled=True)]
    all_to_all x2 -> x0, starting transfers between devices: 12.8 us -> none  [the longest x1 8.11 us: on_device(): lax.all_to_all(send2.reshape(OCC, 16, AREA), 'occ', split_axis=0, concat_...]
    reshape x10 -> x5, local copies, waits for them, and re-layouts: 18 us -> 5.52 us  [the longest x4 5.44 us: finish(): octets.reshape(3, TILE, 8, TILE).transpose(0, 2, 1, 3).reshape(24, AREA)]
    dot_general x2 -> x0, matrix products: 9.33 us -> none  [the longest x1 5.86 us: on_device(): jnp.dot(pick2.astype(jnp.bfloat16), across.reshape(-1, AREA), preferred_e...]
    another operation x5, other arithmetic: 5.54 us -> 1.35 us  [before(): return jnp.cumsum(counts, axis=axis) - counts]
  transfers between devices with their start and end apart: 6 -> 0, of which waited for: 4 -> 0; matrix products, arithmetic and copies ran while one was open for 17% -> 0% of each run, Pallas kernels for 11% -> 0%
where the time goes in v2:
time: 241 us; the launch traced here: 240 us
  Pallas kernels  209 us (87%)
  local copies, waits for them, and re-layouts  21.9 us (9%)
  other arithmetic  8.27 us (3%)
    pallas_call x1, Pallas kernels, main_call(): pl.pallas_call(main_kernel, out_shape=(out, out), in_specs=[pl.BlockSpec(...  194 us
    pallas_call x1, Pallas kernels, marks_call(): pl.pallas_call(marks_kernel, out_shape=jax.ShapeDtypeStruct((OCC, 8, 128)...  14.9 us
    reshape x4, local copies, waits for them, and re-layouts, finish(): octets.reshape(3, TILE, 8, TILE).transpose(0, 2, 1, 3).reshape(24, AREA)  5.44 us

profile of v2, /device:TPU:28, one launch (start us, length us, event | category | flops | bytes accessed | tf_op | source)
XLA Modules:
  0.0 240.3 jit_solution(7423538928226582218)
XLA Ops:
  0.6 0.8 add_bitcast_fusion.2
  1.4 0.1 convert_reduce_fusion
  1.5 0.6 broadcast_in_dim.182.mark_ref
  2.1 14.9 %marks.1 = s32[16,8,128]{2,1,0:T(8,128)} custom-call(s32[8,128]{1,0:T(8,128)} %broadcast_in_dim.182.mark_ref), custom_call_target="tpu_custom_call" | custom-call | tf_op jit(solution)/shard_map/marks/pallas_call | solution.py:66
  17.1 1.0 copy.174
  18.2 0.7 broadcast_compare_fusion.5
  19.1 2.0 multiply_reduce_fusion
  21.1 0.2 reduce_window_sum.55
  21.4 0.1 copy.193
  21.6 0.1 dynamic-slice_compare_fusion
  21.7 0.1 copy.204
  22.4 0.4 fusion.37
  22.9 0.1 copy.177
  23.0 0.8 fusion.38
  23.8 0.1 copy.178
  24.2 0.1 add.454
  24.3 0.2 dynamic-slice_reduce_fusion
  24.6 0.1 mul.230
  24.8 0.4 copy.180
  25.1 0.1 fusion.35
  25.3 0.1 copy.181
  25.4 0.1 reduce_window_sum.51
  25.5 0.9 copy.182
  26.4 0.1 squeeze.27
  26.6 0.2 select_reduce_fusion.1
  26.9 0.1 select_reduce_fusion.7
  27.1 0.2 select_reduce_fusion.2
  27.6 0.2 reduce_window_sum.53
  27.9 0.5 copy.185
  28.7 0.6 select_reduce_fusion.4
  29.4 0.1 broadcast_select_fusion
  29.8 0.1 select_reduce_fusion.3
  30.1 0.1 select_reduce_fusion.5
  30.6 0.2 copy.196
  30.8 0.1 add.520
  30.9 0.2 select_reduce_fusion
  31.4 3.0 %copy.197 = bf16[128,9216]{0,1:T(8,128)(2,1)S(1)} copy(bf16[128,9216]{1,0:T(8,128)(2,1)} %param.7) | data formatting | bytes 4718592 | tf_op args[0]
  34.5 3.2 %copy.199.t_ref = bf16[128,96,96]{2,1,0:T(8,128)(2,1)} copy(bf16[128,96,96]{0,2,1:T(8,128)(2,1)S(1)} %bitcast.64) | data formatting | bytes 4718592 | tf_op jit(solution)/shard_map/reshape | solution.py:429
  37.7 0.6 reshape.605
  38.3 0.9 copy.198
  39.2 1.1 reshape.606.y_ref
  40.3 194.1 %contract.1 = (f32[3,96,768]{2,1,0:T(8,128)}, f32[3,96,768]{2,1,0:T(8,128)}) custom-call(s32[2048]{0:T(1024)} %copy-done.6, bf16[128,96,96]{2,1,0:T(8,128)(2,1)} %copy.199.t_ref, bf16[288,576]{1,0:T(8,128)(2,1)} %x_ref.1, bf16[288,576]{1,0:T(8,128)(2,1)} %reshape.606.y_ref), custom_call_target="tpu_custom_call" | custom-call | flops 1358954496 | bytes 14000000 | tf_op jit(solution)/shard_map/contract/pallas_call | solution.py:293
  234.4 1.7 reshape.607
  236.1 0.2 copy.200
  236.3 1.6 reshape.608
  238.0 0.5 reshape.609
  238.5 0.2 copy.201
  238.7 1.6 reshape.610
  (100 shorter events, 3.4 us)
Async XLA Ops:
  0.6 21.4 %copy-start.3 = (s32[192,3]{0,1:T(4,128)S(1)}, s32[192,3]{0,1:T(4,128)}, u32[]{:S(2)}) copy-start(s32[192,3]{0,1:T(4,128)} %param.11) | copy-start | bytes 6916
  22.8 4.3 %copy-start.2 = (s32[128,3]{0,1:T(4,128)S(1)}, s32[128,3]{0,1:T(4,128)}, u32[]{:S(2)}) copy-start(s32[128,3]{0,1:T(4,128)} %param.8) | copy-start | bytes 4612
  22.8 4.3 %copy-start.4 = (s32[192,3]{0,1:T(4,128)S(1)}, s32[192,3]{0,1:T(4,128)}, u32[]{:S(2)}) copy-start(s32[192,3]{0,1:T(4,128)} %param.10) | copy-start | bytes 6916
  25.1 4.6 %copy-start.5 = (s32[256]{0:T(256)S(1)}, s32[256]{0:T(256)}, u32[]{:S(2)}) copy-start(s32[256]{0:T(256)} %param.9) | copy-start | bytes 3076
  31.4 3.1 %copy-start.6 = (s32[2048]{0:T(1024)}, s32[2048]{0:T(1024)S(1)}, u32[]{:S(2)}) copy-start(s32[2048]{0:T(1024)S(1)} %constant_dynamic-update-slice_fusion.index_ref) | copy-start | bytes 24580
  34.5 3.2 %copy-start.1 = (bf16[576,288]{0,1:T(8,128)(2,1)S(1)}, bf16[576,288]{0,1:T(8,128)(2,1)}, u32[]{:S(2)}) copy-start(bf16[576,288]{0,1:T(8,128)(2,1)} %param.13) | copy-start | bytes 995332
  236.3 1.6 copy-start

commit v3 on v2

v3 whole, which is shorter than its diff:
```python
import functools

import jax
import jax.numpy as jnp
from jax import lax
from jax.experimental import pallas as pl
from jax.experimental.pallas import tpu as pltpu
from jax.sharding import PartitionSpec as P

TILE = 96
NV = 48
AREA = TILE * TILE
OCC = 16
VIR = 8
VT = 6
PAIRS = 16
VCAP = 32
BLOCKS = 288
ROWS = 192
WIDE = 8 * TILE
H = 2
R = TILE // H
FLAT = 144
SUBS = ((0, 80), (80, 64))
MESH = pl.DeviceIdType.MESH
VPACK, LADDER = 0, 256


def main_kernel(
    index_ref, label_ref, rows_ref, t_ref, x_ref, y_ref, ladder_ref, cycle_ref,
    x_got, y_got, blocks, v_send, v_got, v_tiles, o_send, o_got, o_tiles,
    l_part, l_core, l_z, c_part, c_core, c_z,
    v_label, o_label, o_label_got, words, o_index, c_index,
    g_ss, g_rs, v_ss, v_rs, o_ss, o_rs, core_ss, core_rs, z_ss, z_rs,
    vl_ss, vl_rs, ol_ss, ol_rs, w_sem,
):
    occ, vir = lax.axis_index("occ"), lax.axis_index("vir")
    ox, oy = occ // 4, occ % 4
    z, core = vir // 2, vir % 2
    i32 = jnp.int32
    barrier = pltpu.get_barrier_semaphore()
    for k in range(1, VIR):
        pl.semaphore_signal(barrier, inc=1, device_id=(occ, (vir + k) % VIR), device_id_type=MESH)
    for k in range(1, OCC):
        pl.semaphore_signal(barrier, inc=1, device_id=((occ + k) % OCC, vir), device_id_type=MESH)

    pl.semaphore_wait(barrier, VIR + OCC - 2)
    sent = []

    def push(src, dst, ssem, rsem, device):
        copy = pltpu.make_async_remote_copy(src, dst, ssem, rsem, device_id=device, device_id_type=MESH)
        copy.start()
        sent.append(copy)
        return copy

    shards = (x_ref, y_ref)
    landing = (x_got, y_got)
    count = [0, 0]

    def step(rel, axis, k):
        dx, dy = rel // 4, rel % 4
        return ((dx - k) % 4) * 4 + dy if axis == 0 else dx * 4 + (dy - k) % 4

    def target(axis, k):
        return (((ox + k) % 4) * 4 + oy, vir) if axis == 0 else (ox * 4 + (oy + k) % 4, vir)

    def send_sem(array):
        count[array] += 1
        return g_ss.at[array, count[array] - 1]

    def spread(array, axis, rel):
        source = shards[array] if rel == 0 else landing[array].at[rel - 1]
        copies = {}
        for k in (1, 3):
            there = step(rel, axis, k)
            copies[k] = push(
                source, landing[array].at[there - 1], send_sem(array), g_rs.at[array, there - 1, 0], target(axis, k)
            )
        return copies

    def forward(array, axis, rel, copies, flip):
        out = []
        for n, k in enumerate((1, 3)):
            copies[k].wait_recv()
            here = step(rel, axis, k)
            there = step(here, axis, k)
            which = (n + flip) % 2
            rows = pl.ds(*SUBS[which])
            out.append(push(
                landing[array].at[here - 1, rows], landing[array].at[there - 1, rows],
                send_sem(array), g_rs.at[array, there - 1, which], target(axis, k),
            ))
        return out

    first_axis, second_axis = (1, 0), (0, 1)
    first = [spread(array, first_axis[array], 0) for array in range(2)]
    v_labels = [
        push(label_ref.at[k], v_label.at[VIR - k - 1], vl_ss.at[k - 1], vl_rs.at[VIR - k - 1], (occ, (vir + k) % VIR))
        for k in range(1, VIR)
    ]
    second = [{0: spread(array, second_axis[array], 0)} for array in range(2)]
    turned = [[], []]

    def v_pack(q, carry):
        for j in range(8):
            tile = t_ref[index_ref[VPACK + q * 8 + j]]
            for h in range(H):
                v_send[h, q // 4, q % 4, :, j * TILE : (j + 1) * TILE] = tile[h * R : (h + 1) * R]
        return carry

    lax.fori_loop(0, VIR * 4, v_pack, 0)

    def v_push(h):
        return [
            push(v_send.at[h, k], v_got.at[h, VIR - k - 1], v_ss.at[h, k - 1], v_rs.at[h, VIR - k - 1],
                 (occ, (vir + k) % VIR))
            for k in range(1, VIR)
        ]

    v_copies = [v_push(h) for h in range(H)]

    middle = [forward(array, first_axis[array], 0, first[array], 0) for array in range(2)]
    for k in (1, 3):
        for array in range(2):
            rel = step(0, first_axis[array], k)
            second[array][rel] = spread(array, second_axis[array], rel)

    line = lax.broadcasted_iota(i32, (VCAP, 128), 0)
    lane = lax.broadcasted_iota(i32, (VCAP, 128), 1)
    places = [jnp.zeros((VCAP, 128), i32)] * 2
    infos = [jnp.zeros((VCAP, 128), i32)] * 2
    for k in range(VIR):
        if k == 0:
            label = label_ref[0]
        else:
            v_labels[VIR - k - 1].wait_recv()
            label = v_label[k - 1]
        for half in range(2):
            hit = (label >= 0) & ((label & 255) == lane + 128 * half)
            places[half] = places[half] + jnp.where(hit, line + k * VCAP, 0)
            infos[half] = infos[half] + jnp.where(hit, (label >> 8) + 1, 0)
    words[...] = jnp.zeros((16, 128), i32)
    for half in range(2):
        words[half : half + 1] = jnp.minimum(jnp.sum(places[half], axis=0, keepdims=True), VIR * VCAP - 1)
        info = jnp.sum(infos[half].astype(jnp.float32), axis=0, keepdims=True)
        column = jnp.transpose(jnp.broadcast_to(info, (128, 128))).astype(i32)
        o_label[half * 8 : half * 8 + 8] = column.reshape(8, 16, 128)
    to_scalar = pltpu.make_async_copy(words.at[0:8], o_index, w_sem.at[0])
    to_scalar.start()
    o_labels = [
        push(o_label.at[k], o_label_got.at[OCC - k - 1], ol_ss.at[k - 1], ol_rs.at[OCC - k - 1], ((occ + k) % OCC, vir))
        for k in range(1, OCC)
    ]
    to_scalar.wait()

    for array in range(2):
        for copy in middle[array]:
            copy.wait_recv()
        rel = step(step(0, first_axis[array], 1), first_axis[array], 1)
        second[array][rel] = spread(array, second_axis[array], rel)
    blocks[BLOCKS] = jnp.zeros((TILE, TILE), jnp.bfloat16)
    for n in range(4):
        for array in range(2):
            rel = list(second[array])[n]
            turned[array] = turned[array] + forward(array, second_axis[array], rel, second[array][rel], n % 2)

    def gather_unpack(array):
        for copy in turned[array]:
            copy.wait_recv()

        def unpack_from(ref, base):
            left, right = ref[:, : 6 * TILE], ref[:, 6 * TILE :]
            strips = (left[:TILE], jnp.concatenate([left[TILE:], right[: 2 * TILE - FLAT]], axis=0), right[2 * TILE - FLAT :])
            for row in range(3):
                for c in range(6):
                    blocks[base + row * 6 + c] = strips[row][:, c * TILE : (c + 1) * TILE]

        unpack_from(shards[array], 0)

        def body(n, carry):
            unpack_from(landing[array].at[n], (n + 1) * 18)
            return carry

        lax.fori_loop(0, OCC - 1, body, 0)

    def cycle_words():
        line16 = lax.broadcasted_iota(i32, (16, 128), 0)
        totals = [jnp.zeros((16, 128), i32)] * 2
        for k in range(OCC):
            if k == 0:
                label = o_label[0]
            else:
                o_labels[OCC - k - 1].wait_recv()
                label = o_label_got[k - 1]
            value = (line16 + k * 16) * 8 + ((label - 1) & 7) + 1
            for half in range(2):
                hit = (label > 0) & (rows_ref[half, 0:1] == k) & (((label - 1) >> 3) == rows_ref[half, 1:2])
                totals[half] = totals[half] + jnp.where(hit, value, 0)
        for half in range(2):
            for j in range(2):
                found = jnp.sum(totals[half][j * 8 : j * 8 + 8], axis=0, keepdims=True)
                block = jnp.where(found > 0, rows_ref[half, 2:3] + 3 * ((found - 1) & 7), BLOCKS)
                tile = jnp.where(found > 0, (found - 1) >> 3, 0)
                words[8 + half * 4 + j : 9 + half * 4 + j] = jnp.clip(block, 0, BLOCKS)
                words[10 + half * 4 + j : 11 + half * 4 + j] = jnp.minimum(tile, 255)
        copy = pltpu.make_async_copy(words.at[8:16], c_index, w_sem.at[1])
        copy.start()
        copy.wait()

    def split(dst, strip, base):
        for j in range(8):
            dst[base + j] = strip[:, j * TILE : (j + 1) * TILE]

    def o_step(h):
        for copy in v_copies[h]:
            copy.wait_recv()
        for q in range(4):
            split(v_tiles, v_send[h, 0, q], q * 8)

        def unpack(q, carry):
            split(v_tiles, v_got[h, q // 4, q % 4], (q + 4) * 8)
            return carry

        lax.fori_loop(0, (VIR - 1) * 4, unpack, 0)

        def pack(q, carry):
            for j in range(8):
                o_send[h, q // 2, q % 2, :, j * TILE : (j + 1) * TILE] = v_tiles[o_index[q // 16, (q % 16) * 8 + j]]
            return carry

        lax.fori_loop(0, OCC * 2, pack, 0)
        return [
            push(o_send.at[h, k], o_got.at[h, OCC - k - 1], o_ss.at[h, k - 1], o_rs.at[h, OCC - k - 1],
                 ((occ + k) % OCC, vir))
            for k in range(1, OCC)
        ]

    def products(look, tiles, part, swap):
        def octet(q, carry):
            owner = q // 3
            for j in range(8):
                row = q * 8 + j
                total = None
                for half in range(2):
                    block = blocks[look(half, row)]
                    tile = tiles[look(2 + half, row)]
                    left, right = (tile, block) if swap else (block, tile)
                    term = jnp.dot(left, right, preferred_element_type=jnp.float32)
                    total = term if total is None else total + term
                part[owner % 2, owner // 2, q % 3, :, j * TILE : (j + 1) * TILE] = total.astype(jnp.bfloat16)
            return carry

        lax.fori_loop(0, ROWS // 8, octet, 0)

    def core_push(n, part, dst):
        return push(part.at[1 - core], dst, core_ss.at[n], core_rs.at[n], (occ, z * 2 + 1 - core))

    def z_push(n, copy, part, dst, z_got):
        copy.wait_recv()

        def add(q, carry):
            total = part[core, q // 3, q % 3].astype(jnp.float32) + dst[q // 3, q % 3].astype(jnp.float32)
            dst[q // 3, q % 3] = total.astype(jnp.bfloat16)
            return carry

        lax.fori_loop(0, 12, add, 0)
        return [
            push(dst.at[(z + k) % 4], z_got.at[4 - k - 1], z_ss.at[n, k - 1], z_rs.at[n, 4 - k - 1],
                 (occ, ((z + k) % 4) * 2 + core))
            for k in (1, 3, 2)
        ]

    def finish(copies, dst, z_got, out, first, rows):
        for copy in copies:
            copy.wait_recv()
        for i in range(3):
            total = dst[z, i].astype(jnp.float32)
            for k in range(3):
                total = total + z_got[k, i].astype(jnp.float32)
            out[i, first : first + rows] = total

    o_copies = [o_step(h) for h in range(H)]
    gather_unpack(0)
    products(lambda n, row: index_ref[LADDER + n * ROWS + row], t_ref, l_part, False)
    l_copy = core_push(H, l_part, l_core)
    cycle_words()
    gather_unpack(1)
    l_copies = z_push(H, l_copy, l_part, l_core, l_z)
    c_copies = []
    for h in range(H):
        for copy in o_copies[h]:
            copy.wait_recv()
        for j in range(2):
            split(o_tiles, o_send[h, 0, j], j * 8)

        def unpack(q, carry):
            split(o_tiles, o_got[h, q // 2, q % 2], (q + 2) * 8)
            return carry

        lax.fori_loop(0, (OCC - 1) * 2, unpack, 0)
        products(lambda n, row: c_index[(row // 128) * 4 + n, row % 128], o_tiles, c_part.at[h], True)
        c_copies.append(core_push(h, c_part.at[h], c_core.at[h]))
        if h > 0:
            c_copies[h - 1] = z_push(h - 1, c_copies[h - 1], c_part.at[h - 1], c_core.at[h - 1], c_z.at[h - 1])
    c_copies[H - 1] = z_push(H - 1, c_copies[H - 1], c_part.at[H - 1], c_core.at[H - 1], c_z.at[H - 1])
    finish(l_copies, l_core, l_z, ladder_ref, 0, TILE)
    for h in range(H):
        finish(c_copies[h], c_core.at[h], c_z.at[h], cycle_ref, h * R, R)
    for copy in sent:
        copy.wait_send()


def main_call(index, labels, rows, tiles, x, y):
    bf16 = jnp.bfloat16
    vmem = pl.BlockSpec(memory_space=pltpu.VMEM)
    dma = pltpu.SemaphoreType.DMA
    out = jax.ShapeDtypeStruct((3, TILE, WIDE), jnp.float32)
    return pl.pallas_call(
        main_kernel,
        out_shape=(out, out),
        in_specs=[pl.BlockSpec(memory_space=pltpu.SMEM)] + [vmem] * 5,
        out_specs=(vmem, vmem),
        scratch_shapes=[
            pltpu.VMEM((OCC - 1, FLAT, 12 * TILE), bf16),
            pltpu.VMEM((OCC - 1, FLAT, 12 * TILE), bf16),
            pltpu.VMEM((BLOCKS + 1, TILE, TILE), bf16),
            pltpu.VMEM((H, VIR, 4, R, WIDE), bf16),
            pltpu.VMEM((H, VIR - 1, 4, R, WIDE), bf16),
            pltpu.VMEM((256, R, TILE), bf16),
            pltpu.VMEM((H, OCC, 2, R, WIDE), bf16),
            pltpu.VMEM((H, OCC - 1, 2, R, WIDE), bf16),
            pltpu.VMEM((256, R, TILE), bf16),
            pltpu.VMEM((2, 4, 3, TILE, WIDE), bf16),
            pltpu.VMEM((4, 3, TILE, WIDE), bf16),
            pltpu.VMEM((3, 3, TILE, WIDE), bf16),
            pltpu.VMEM((H, 2, 4, 3, R, WIDE), bf16),
            pltpu.VMEM((H, 4, 3, R, WIDE), bf16),
            pltpu.VMEM((H, 3, 3, R, WIDE), bf16),
            pltpu.VMEM((VIR - 1, VCAP, 128), jnp.int32),
            pltpu.VMEM((OCC, 16, 128), jnp.int32),
            pltpu.VMEM((OCC - 1, 16, 128), jnp.int32),
            pltpu.VMEM((16, 128), jnp.int32),
            pltpu.SMEM((8, 128), jnp.int32),
            pltpu.SMEM((8, 128), jnp.int32),
            dma((2, 20)), dma((2, OCC - 1, 2)),
            dma((H, VIR - 1)), dma((H, VIR - 1)),
            dma((H, OCC - 1)), dma((H, OCC - 1)),
            dma((H + 1,)), dma((H + 1,)),
            dma((H + 1, 3)), dma((H + 1, 3)),
            dma((VIR - 1,)), dma((VIR - 1,)), dma((OCC - 1,)), dma((OCC - 1,)), dma((2,)),
        ],
        compiler_params=pltpu.CompilerParams(
            collective_id=1, has_side_effects=True, vmem_limit_bytes=63_000_000
        ),
        cost_estimate=pl.CostEstimate(flops=8 * ROWS * TILE**3, bytes_accessed=14_000_000, transcendentals=0),
        name="contract",
    )(index, labels, rows, tiles, x, y)


def lookup(ids, table):
    flat = table.reshape(-1)
    hits = ids[..., None] == jnp.arange(flat.shape[0], dtype=jnp.int32)
    return jnp.sum(jnp.where(hits, flat, 0), axis=-1)


def before(counts, axis):
    return jnp.cumsum(counts, axis=axis) - counts


def on_device(t_tiles, t_index, cycle_map, ladder_slots, cycle_slots, x_ints, y_ints):
    occ = lax.axis_index("occ")
    vir = lax.axis_index("vir")
    i32 = jnp.int32
    local = t_index[:, 0] - occ * PAIRS
    first = t_index[:, 1] - vir * VT
    second = t_index[:, 2]
    pair_range = jnp.arange(2, dtype=i32)
    vir_range = jnp.arange(VIR, dtype=i32)

    marks = jnp.arange(PAIRS * NV, dtype=i32)[None, :] == (local * NV + second)[:, None]
    domain = jnp.max(marks.astype(i32), axis=0).reshape(PAIRS, VIR, VT)
    counts = jnp.sum(domain, axis=-1)
    rank_in = before(domain, 2)
    rank_all = rank_in + before(counts, 1)[..., None]
    own_counts = lax.dynamic_index_in_dim(counts, vir, 1, keepdims=True)
    starts = before(own_counts * counts, 0)

    send_table = ((vir_range - vir) % VIR)[None, :, None] * VCAP + starts[:, :, None] + rank_in * own_counts[:, :, None]
    by_second = lookup(local * NV + second, send_table * 2 + rank_in)
    to_group = (lax.dynamic_slice_in_dim(cycle_map, occ * PAIRS, PAIRS, 0) - occ) % OCC
    own_rank = lax.dynamic_index_in_dim(rank_in, vir, 1, keepdims=False)
    own_all = lax.dynamic_index_in_dim(rank_all, vir, 1, keepdims=False)
    by_first = lookup(local * VT + first, own_rank + 2 * own_all + 16 * to_group[:, None])
    which = by_first % 2
    position = by_second // 2 + which
    target = (by_first // 16) * 16 + (by_second % 2) * 8 + (by_first // 2) % 8
    label = target + 256 * (t_index[:, 1] * 8 + second % VT)
    pick = jnp.arange(VIR * VCAP, dtype=i32)[:, None] == position[None, :]
    packed_pick = jnp.sum(jnp.where(pick, label * 128 + jnp.arange(128, dtype=i32) + 1, 0), axis=1)
    v_pack = jnp.where(packed_pick > 0, (packed_pick - 1) % 128, 0)
    labels = jnp.where(packed_pick > 0, (packed_pick - 1) // 128, -1)
    labels = jnp.broadcast_to(labels.reshape(VIR, VCAP, 1), (VIR, VCAP, 128))

    def ahead(group):
        return ((group // 4 - occ // 4) % 4) * 4 + (group % 4 - occ % 4) % 4

    tile_key = (local * 2 + which) * NV + second
    row_key = (ladder_slots[:, 0][None, :] * 2 + pair_range[:, None]) * NV + ladder_slots[:, 2][None, :]
    match = row_key[:, :, None] == tile_key[None, None, :]
    packed = jnp.arange(128, dtype=i32) * 8 + first + 1
    found = jnp.sum(jnp.where(match, packed, 0), axis=-1)
    ladder_tile = jnp.where(found > 0, (found - 1) // 8, 0)
    x_row = ladder_slots[:, 1]
    x_block = (ahead(x_row // 3) * 3 + x_row % 3) * VT
    ladder_block = jnp.where(found > 0, x_block[None, :] + (found - 1) % 8, BLOCKS)

    by_o = (cycle_map.reshape(OCC, PAIRS) == occ).astype(i32)
    ahead_of = jnp.sum(by_o * ((jnp.arange(OCC, dtype=i32) - occ) % OCC)[:, None], axis=0)
    s, a, b = cycle_slots[:, 0], cycle_slots[:, 1], cycle_slots[:, 2]
    rows = jnp.stack([lookup(s, ahead_of), a, ahead(b // 3) * 18 + b % 3], axis=0)
    rows = jnp.pad(rows, ((0, 5), (0, 256 - ROWS)), constant_values=-1).reshape(8, 2, 128).transpose(1, 0, 2)

    index = jnp.concatenate([v_pack, ladder_block.reshape(-1), ladder_tile.reshape(-1)])
    x_flat = jnp.concatenate([x_ints[:FLAT], x_ints[FLAT:]], axis=1)
    y_rows = y_ints.reshape(3, 2, TILE, 3, TILE).transpose(0, 2, 1, 3, 4).reshape(3 * TILE, 6 * TILE)
    y_flat = jnp.concatenate([y_rows[:FLAT], y_rows[FLAT:]], axis=1)
    ladder, cycle = main_call(index, labels, rows, t_tiles.reshape(128, TILE, TILE), x_flat, y_flat)

    def finish(octets):
        return octets.reshape(3, TILE, 8, TILE).transpose(0, 2, 1, 3).reshape(24, AREA)

    return finish(ladder), finish(cycle)


def solution(mesh):
    return jax.shard_map(
        on_device,
        mesh=mesh,
        in_specs=(
            P(("occ", "vir"), None),
            P(("occ", "vir"), None),
            P(),
            P("occ", None),
            P("occ", None),
            P("occ", "vir"),
            P("vir", "occ"),
        ),
        out_specs=(P(("occ", "vir"), None), P(("occ", "vir"), None)),
        check_vma=False,
    )
```

time: 241 us -> 205 us (0.85)
  Pallas kernels: 209 us -> 176 us
  local copies, waits for them, and re-layouts: 21.9 us -> 17.1 us
    pallas_call x1, Pallas kernels: 194 us -> 176 us  [main_call(): pl.pallas_call(main_kernel, out_shape=(out, out), in_specs=[pl.BlockSpec(...]
    pallas_call x1 -> x0, Pallas kernels: 14.9 us -> none  [marks_call(): pl.pallas_call(marks_kernel, out_shape=jax.ShapeDtypeStruct((OCC, 8, 128)...]
    slice x4 -> x3, local copies, waits for them, and re-layouts: 2.73 us -> 0.07 us  [the longest x1 0.03 us: on_device(): y_flat = jnp.concatenate([y_rows[:FLAT], y_rows[FLAT:]], axis=1)]
    reduce_sum x5 -> x2, other arithmetic: 2.95 us -> 0.45 us  [the longest x1 0.34 us: on_device(): counts = jnp.sum(domain, axis=-1)]
where the time goes in v3:
time: 205 us; the launch traced here: 204 us
  Pallas kernels  176 us (86%)
  local copies, waits for them, and re-layouts  17.1 us (8%)
  other arithmetic  9.91 us (5%)
    pallas_call x1, Pallas kernels, main_call(): pl.pallas_call(main_kernel, out_shape=(out, out), in_specs=[pl.BlockSpec(...  176 us
    reshape x4, local copies, waits for them, and re-layouts, finish(): octets.reshape(3, TILE, 8, TILE).transpose(0, 2, 1, 3).reshape(24, AREA)  5.44 us

profile of v3, /device:TPU:28, one launch (start us, length us, event | category | flops | bytes accessed | tf_op | source)
XLA Modules:
  0.0 203.9 jit_solution(9938394956695096433)
XLA Ops:
  0.7 0.8 add_bitcast_fusion
  1.5 0.1 convert_reduce_fusion
  1.6 0.1 reshape.590
  1.7 2.5 %reduce_window_sum.36 = s32[16,8,6]{2,1,0:T(8,128)S(1)} reduce-window(s32[16,8,6]{2,1,0:T(8,128)S(1)} %reshape.590, s32[]{:T(128)} %constant.275.clone.1), window={size=1x1x6 pad=0_0x0_0x5_0}, to_apply=%region_3.4 | reduce-window | flops 3840 | bytes 6148 | tf_op jit(solution)/shard_map/jit(cumsum)/reduce_window_sum | solution.py:367
  4.3 0.3 fusion.40
  4.6 0.2 dynamic-slice_reduce_fusion
  4.8 0.2 reduce_window_sum.38
  5.0 0.1 broadcast_multiply_fusion
  5.1 0.1 add_reduce_fusion
  5.2 0.1 add.406
  5.3 0.8 and_select_fusion.5
  6.1 0.1 add.410
  6.2 0.1 select_reduce_fusion.3
  6.4 0.1 add.398
  6.5 0.1 add.399
  6.6 0.1 mul.208
  6.7 0.1 mul.209
  6.9 0.1 reduce_window_sum.37
  7.0 0.2 select_reduce_fusion
  7.2 0.8 add_add_fusion
  8.0 0.8 broadcast_divide_fusion
  8.8 0.2 select_reduce_fusion.1
  9.1 0.1 gt.22
  9.2 0.7 compare_reduce_fusion
  10.0 0.1 add.442
  10.1 0.1 sub.199
  10.2 0.1 select_reduce_fusion.2
  10.3 0.6 pad_add_fusion.index_ref
  10.9 0.1 gt.23
  11.0 0.1 sub.201
  11.1 0.8 broadcast_in_dim.81.label_ref
  11.9 0.1 eq.139
  12.0 0.1 select_reduce_fusion.5
  12.1 0.1 select_reduce_fusion.4
  12.2 0.6 pad_bitcast_fusion.rows_ref
  12.8 3.0 %copy.18 = bf16[128,9216]{0,1:T(8,128)(2,1)S(1)} copy(bf16[128,9216]{1,0:T(8,128)(2,1)} %param.7) | data formatting | bytes 4718592 | tf_op args[0]
  15.8 3.2 %copy.20.t_ref = bf16[128,96,96]{2,1,0:T(8,128)(2,1)} copy(bf16[128,96,96]{0,2,1:T(8,128)(2,1)S(1)} %bitcast.66) | data formatting | bytes 4718592 | tf_op jit(solution)/shard_map/reshape | solution.py:427
  19.1 0.6 reshape.593
  19.7 0.9 copy.19
  20.6 0.4 reshape.594
  21.0 1.0 pad_maximum_fusion
  22.0 175.9 %contract.1 = (f32[3,96,768]{2,1,0:T(8,128)}, f32[3,96,768]{2,1,0:T(8,128)}) custom-call(s32[1024]{0:T(1024)} %pad_add_fusion.index_ref, s32[8,32,128]{2,1,0:T(8,128)} %broadcast_in_dim.81.label_ref, s32[2,8,128]{2,1,0:T(8,128)} %pad_bitcast_fusion.rows_ref, bf16[128,96,96]{2,1,0:T(8,128)(2,1)} %copy.20.t_ref, bf16[144,1152]{1,0:T(8,128)(2,1)} %get-tuple-element.33.x_ref, ...), custom_call_target="tpu_custom_call" | custom-call | flops 1358954496 | bytes 14000000 | tf_op jit(solution)/shard_map/contract/pallas_call | solution.py:318
  198.0 1.7 reshape.595
  199.7 0.2 copy.21
  199.9 1.6 reshape.596
  201.5 0.5 reshape.597
  202.1 0.2 copy.22
  202.3 1.6 reshape.598
  (31 shorter events, 0.5 us)
Async XLA Ops:
  0.6 11.2 %copy-start.4 = (s32[256]{0:T(256)S(1)}, s32[256]{0:T(256)}, u32[]{:S(2)}) copy-start(s32[256]{0:T(256)} %param.9) | copy-start | bytes 3076
  0.6 11.2 %copy-start.3 = (s32[192,3]{0,1:T(4,128)S(1)}, s32[192,3]{0,1:T(4,128)}, u32[]{:S(2)}) copy-start(s32[192,3]{0,1:T(4,128)} %param.11) | copy-start | bytes 6916
  15.8 3.2 %copy-start.1 = (bf16[288,576]{1,0:T(8,128)(2,1)S(1)}, bf16[288,576]{1,0:T(8,128)(2,1)}, u32[]{:S(2)}) copy-start(bf16[288,576]{1,0:T(8,128)(2,1)} %param.12) | copy-start | bytes 995332
  15.8 3.2 %copy-start.2 = (bf16[576,288]{0,1:T(8,128)(2,1)S(1)}, bf16[576,288]{0,1:T(8,128)(2,1)}, u32[]{:S(2)}) copy-start(bf16[576,288]{0,1:T(8,128)(2,1)} %param.13) | copy-start | bytes 995332
  199.9 1.6 copy-start

commit v4 on v3

--- a/solution.py
+++ b/solution.py
@@ -18,8 +18,9 @@
 BLOCKS = 288
 ROWS = 192
 WIDE = 8 * TILE
-H = 2
-R = TILE // H
+CHUNKS = ((0, 32), (32, 32), (64, 32))
+H = len(CHUNKS)
+MOST = max(n for _, n in CHUNKS)
 FLAT = 144
 SUBS = ((0, 80), (80, 64))
 MESH = pl.DeviceIdType.MESH
@@ -28,7 +29,7 @@
 
 def main_kernel(
     index_ref, label_ref, rows_ref, t_ref, x_ref, y_ref, ladder_ref, cycle_ref,
-    x_got, y_got, blocks, v_send, v_got, v_tiles, o_send, o_got, o_tiles,
+    x_flat, y_flat, x_got, y_got, blocks, v_send, v_got, o_send, o_got, small,
     l_part, l_core, l_z, c_part, c_core, c_z,
     v_label, o_label, o_label_got, words, o_index, c_index,
     g_ss, g_rs, v_ss, v_rs, o_ss, o_rs, core_ss, core_rs, z_ss, z_rs,
@@ -44,6 +45,14 @@
     for k in range(1, OCC):
         pl.semaphore_signal(barrier, inc=1, device_id=((occ + k) % OCC, vir), device_id_type=MESH)
 
+    for part in range(2):
+        x_flat[:, part * 6 * TILE : (part + 1) * 6 * TILE] = x_ref[part * FLAT : (part + 1) * FLAT]
+    for d in range(6):
+        first_row, lane = (d // 2) * TILE, (d % 2) * 3 * TILE
+        for start in range(0, TILE, 48):
+            row = first_row + start
+            shift = (row // FLAT) * 6 * TILE + lane
+            y_flat[row % FLAT : row % FLAT + 48, shift : shift + 3 * TILE] = y_ref[d * TILE + start : d * TILE + start + 48]
     pl.semaphore_wait(barrier, VIR + OCC - 2)
     sent = []
 
@@ -53,7 +62,7 @@
         sent.append(copy)
         return copy
 
-    shards = (x_ref, y_ref)
+    shards = (x_flat, y_flat)
     landing = (x_got, y_got)
     count = [0, 0]
 
@@ -104,15 +113,17 @@
     def v_pack(q, carry):
         for j in range(8):
             tile = t_ref[index_ref[VPACK + q * 8 + j]]
-            for h in range(H):
-                v_send[h, q // 4, q % 4, :, j * TILE : (j + 1) * TILE] = tile[h * R : (h + 1) * R]
+            v_send[q // 4, q % 4, :, j * TILE : (j + 1) * TILE] = tile
         return carry
 
     lax.fori_loop(0, VIR * 4, v_pack, 0)
+
+    def rows(h):
+        return pl.ds(*CHUNKS[h])
 
     def v_push(h):
         return [
-            push(v_send.at[h, k], v_got.at[h, VIR - k - 1], v_ss.at[h, k - 1], v_rs.at[h, VIR - k - 1],
+            push(v_send.at[k, :, rows(h)], v_got.at[VIR - k - 1, :, rows(h)], v_ss.at[h, k - 1], v_rs.at[h, VIR - k - 1],
                  (occ, (vir + k) % VIR))
             for k in range(1, VIR)
         ]
@@ -214,28 +225,29 @@
     def o_step(h):
         for copy in v_copies[h]:
             copy.wait_recv()
+        tiles = small.at[:, pl.ds(0, CHUNKS[h][1])]
         for q in range(4):
-            split(v_tiles, v_send[h, 0, q], q * 8)
+            split(tiles, v_send[0, q, rows(h)], q * 8)
 
         def unpack(q, carry):
-            split(v_tiles, v_got[h, q // 4, q % 4], (q + 4) * 8)
+            split(tiles, v_got[q // 4, q % 4, rows(h)], (q + 4) * 8)
             return carry
 
         lax.fori_loop(0, (VIR - 1) * 4, unpack, 0)
 
         def pack(q, carry):
             for j in range(8):
-                o_send[h, q // 2, q % 2, :, j * TILE : (j + 1) * TILE] = v_tiles[o_index[q // 16, (q % 16) * 8 + j]]
+                o_send[q // 2, q % 2, rows(h), j * TILE : (j + 1) * TILE] = tiles[o_index[q // 16, (q % 16) * 8 + j]]
             return carry
 
         lax.fori_loop(0, OCC * 2, pack, 0)
         return [
-            push(o_send.at[h, k], o_got.at[h, OCC - k - 1], o_ss.at[h, k - 1], o_rs.at[h, OCC - k - 1],
-                 ((occ + k) % OCC, vir))
+            push(o_send.at[k, :, rows(h)], o_got.at[OCC - k - 1, :, rows(h)], o_ss.at[h, k - 1],
+                 o_rs.at[h, OCC - k - 1], ((occ + k) % OCC, vir))
             for k in range(1, OCC)
         ]
 
-    def products(look, tiles, part, swap):
+    def products(look, tiles, part, held, swap):
         def octet(q, carry):
             owner = q // 3
             for j in range(8):
@@ -247,65 +259,68 @@
                     left, right = (tile, block) if swap else (block, tile)
                     term = jnp.dot(left, right, preferred_element_type=jnp.float32)
                     total = term if total is None else total + term
-                part[owner % 2, owner // 2, q % 3, :, j * TILE : (j + 1) * TILE] = total.astype(jnp.bfloat16)
+                part[owner % 2, owner // 2, q % 3, held, j * TILE : (j + 1) * TILE] = total.astype(jnp.bfloat16)
             return carry
 
         lax.fori_loop(0, ROWS // 8, octet, 0)
 
-    def core_push(n, part, dst):
-        return push(part.at[1 - core], dst, core_ss.at[n], core_rs.at[n], (occ, z * 2 + 1 - core))
-
-    def z_push(n, copy, part, dst, z_got):
+    def core_push(n, part, dst, held):
+        return push(part.at[1 - core, :, :, held], dst.at[:, :, held], core_ss.at[n], core_rs.at[n], (occ, z * 2 + 1 - core))
+
+    def z_push(n, copy, part, dst, z_got, held):
         copy.wait_recv()
 
         def add(q, carry):
-            total = part[core, q // 3, q % 3].astype(jnp.float32) + dst[q // 3, q % 3].astype(jnp.float32)
-            dst[q // 3, q % 3] = total.astype(jnp.bfloat16)
+            total = part[core, q // 3, q % 3, held].astype(jnp.float32) + dst[q // 3, q % 3, held].astype(jnp.float32)
+            dst[q // 3, q % 3, held] = total.astype(jnp.bfloat16)
             return carry
 
         lax.fori_loop(0, 12, add, 0)
         return [
-            push(dst.at[(z + k) % 4], z_got.at[4 - k - 1], z_ss.at[n, k - 1], z_rs.at[n, 4 - k - 1],
+            push(dst.at[(z + k) % 4, :, held], z_got.at[4 - k - 1, :, held], z_ss.at[n, k - 1], z_rs.at[n, 4 - k - 1],
                  (occ, ((z + k) % 4) * 2 + core))
             for k in (1, 3, 2)
         ]
 
-    def finish(copies, dst, z_got, out, first, rows):
+    def finish(copies, dst, z_got, out, held):
         for copy in copies:
             copy.wait_recv()
         for i in range(3):
-            total = dst[z, i].astype(jnp.float32)
+            total = dst[z, i, held].astype(jnp.float32)
             for k in range(3):
-                total = total + z_got[k, i].astype(jnp.float32)
-            out[i, first : first + rows] = total
-
+                total = total + z_got[k, i, held].astype(jnp.float32)
+            for j in range(8):
+                out[i * 8 + j, held] = total[:, j * TILE : (j + 1) * TILE]
+
+    whole = pl.ds(0, TILE)
     o_copies = [o_step(h) for h in range(H)]
     gather_unpack(0)
-    products(lambda n, row: index_ref[LADDER + n * ROWS + row], t_ref, l_part, False)
-    l_copy = core_push(H, l_part, l_core)
+    products(lambda n, row: index_ref[LADDER + n * ROWS + row], t_ref, l_part, whole, False)
+    l_copy = core_push(H, l_part, l_core, whole)
     cycle_words()
     gather_unpack(1)
-    l_copies = z_push(H, l_copy, l_part, l_core, l_z)
+    l_copies = z_push(H, l_copy, l_part, l_core, l_z, whole)
     c_copies = []
     for h in range(H):
         for copy in o_copies[h]:
             copy.wait_recv()
+        tiles = small.at[:, pl.ds(0, CHUNKS[h][1])]
         for j in range(2):
-            split(o_tiles, o_send[h, 0, j], j * 8)
+            split(tiles, o_send[0, j, rows(h)], j * 8)
 
         def unpack(q, carry):
-            split(o_tiles, o_got[h, q // 2, q % 2], (q + 2) * 8)
+            split(tiles, o_got[q // 2, q % 2, rows(h)], (q + 2) * 8)
             return carry
 
         lax.fori_loop(0, (OCC - 1) * 2, unpack, 0)
-        products(lambda n, row: c_index[(row // 128) * 4 + n, row % 128], o_tiles, c_part.at[h], True)
-        c_copies.append(core_push(h, c_part.at[h], c_core.at[h]))
+        products(lambda n, row: c_index[(row // 128) * 4 + n, row % 128], tiles, c_part, rows(h), True)
+        c_copies.append(core_push(h, c_part, c_core, rows(h)))
         if h > 0:
-            c_copies[h - 1] = z_push(h - 1, c_copies[h - 1], c_part.at[h - 1], c_core.at[h - 1], c_z.at[h - 1])
-    c_copies[H - 1] = z_push(H - 1, c_copies[H - 1], c_part.at[H - 1], c_core.at[H - 1], c_z.at[H - 1])
-    finish(l_copies, l_core, l_z, ladder_ref, 0, TILE)
+            c_copies[h - 1] = z_push(h - 1, c_copies[h - 1], c_part, c_core, c_z, rows(h - 1))
+    finish(l_copies, l_core, l_z, ladder_ref, whole)
+    c_copies[H - 1] = z_push(H - 1, c_copies[H - 1], c_part, c_core, c_z, rows(H - 1))
     for h in range(H):
-        finish(c_copies[h], c_core.at[h], c_z.at[h], cycle_ref, h * R, R)
+        finish(c_copies[h], c_core, c_z, cycle_ref, rows(h))
     for copy in sent:
         copy.wait_send()
 
@@ -314,28 +329,29 @@
     bf16 = jnp.bfloat16
     vmem = pl.BlockSpec(memory_space=pltpu.VMEM)
     dma = pltpu.SemaphoreType.DMA
-    out = jax.ShapeDtypeStruct((3, TILE, WIDE), jnp.float32)
+    out = jax.ShapeDtypeStruct((24, TILE, TILE), jnp.float32)
     return pl.pallas_call(
         main_kernel,
         out_shape=(out, out),
         in_specs=[pl.BlockSpec(memory_space=pltpu.SMEM)] + [vmem] * 5,
         out_specs=(vmem, vmem),
         scratch_shapes=[
+            pltpu.VMEM((FLAT, 12 * TILE), bf16),
+            pltpu.VMEM((FLAT, 12 * TILE), bf16),
             pltpu.VMEM((OCC - 1, FLAT, 12 * TILE), bf16),
             pltpu.VMEM((OCC - 1, FLAT, 12 * TILE), bf16),
             pltpu.VMEM((BLOCKS + 1, TILE, TILE), bf16),
-            pltpu.VMEM((H, VIR, 4, R, WIDE), bf16),
-            pltpu.VMEM((H, VIR - 1, 4, R, WIDE), bf16),
-            pltpu.VMEM((256, R, TILE), bf16),
-            pltpu.VMEM((H, OCC, 2, R, WIDE), bf16),
-            pltpu.VMEM((H, OCC - 1, 2, R, WIDE), bf16),
-            pltpu.VMEM((256, R, TILE), bf16),
+            pltpu.VMEM((VIR, 4, TILE, WIDE), bf16),
+            pltpu.VMEM((VIR - 1, 4, TILE, WIDE), bf16),
+            pltpu.VMEM((OCC, 2, TILE, WIDE), bf16),
+            pltpu.VMEM((OCC - 1, 2, TILE, WIDE), bf16),
+            pltpu.VMEM((256, MOST, TILE), bf16),
             pltpu.VMEM((2, 4, 3, TILE, WIDE), bf16),
             pltpu.VMEM((4, 3, TILE, WIDE), bf16),
             pltpu.VMEM((3, 3, TILE, WIDE), bf16),
-            pltpu.VMEM((H, 2, 4, 3, R, WIDE), bf16),
-            pltpu.VMEM((H, 4, 3, R, WIDE), bf16),
-            pltpu.VMEM((H, 3, 3, R, WIDE), bf16),
+            pltpu.VMEM((2, 4, 3, TILE, WIDE), bf16),
+            pltpu.VMEM((4, 3, TILE, WIDE), bf16),
+            pltpu.VMEM((3, 3, TILE, WIDE), bf16),
             pltpu.VMEM((VIR - 1, VCAP, 128), jnp.int32),
             pltpu.VMEM((OCC, 16, 128), jnp.int32),
             pltpu.VMEM((OCC - 1, 16, 128), jnp.int32),
@@ -357,44 +373,34 @@
     )(index, labels, rows, tiles, x, y)
 
 
-def lookup(ids, table):
-    flat = table.reshape(-1)
-    hits = ids[..., None] == jnp.arange(flat.shape[0], dtype=jnp.int32)
-    return jnp.sum(jnp.where(hits, flat, 0), axis=-1)
-
-
-def before(counts, axis):
-    return jnp.cumsum(counts, axis=axis) - counts
-
-
 def on_device(t_tiles, t_index, cycle_map, ladder_slots, cycle_slots, x_ints, y_ints):
     occ = lax.axis_index("occ")
     vir = lax.axis_index("vir")
     i32 = jnp.int32
+    pair_range = jnp.arange(2, dtype=i32)
     local = t_index[:, 0] - occ * PAIRS
-    first = t_index[:, 1] - vir * VT
+    first = t_index[:, 1]
     second = t_index[:, 2]
-    pair_range = jnp.arange(2, dtype=i32)
-    vir_range = jnp.arange(VIR, dtype=i32)
-
-    marks = jnp.arange(PAIRS * NV, dtype=i32)[None, :] == (local * NV + second)[:, None]
-    domain = jnp.max(marks.astype(i32), axis=0).reshape(PAIRS, VIR, VT)
-    counts = jnp.sum(domain, axis=-1)
-    rank_in = before(domain, 2)
-    rank_all = rank_in + before(counts, 1)[..., None]
-    own_counts = lax.dynamic_index_in_dim(counts, vir, 1, keepdims=True)
-    starts = before(own_counts * counts, 0)
-
-    send_table = ((vir_range - vir) % VIR)[None, :, None] * VCAP + starts[:, :, None] + rank_in * own_counts[:, :, None]
-    by_second = lookup(local * NV + second, send_table * 2 + rank_in)
-    to_group = (lax.dynamic_slice_in_dim(cycle_map, occ * PAIRS, PAIRS, 0) - occ) % OCC
-    own_rank = lax.dynamic_index_in_dim(rank_in, vir, 1, keepdims=False)
-    own_all = lax.dynamic_index_in_dim(rank_all, vir, 1, keepdims=False)
-    by_first = lookup(local * VT + first, own_rank + 2 * own_all + 16 * to_group[:, None])
-    which = by_first % 2
-    position = by_second // 2 + which
-    target = (by_first // 16) * 16 + (by_second % 2) * 8 + (by_first // 2) % 8
-    label = target + 256 * (t_index[:, 1] * 8 + second % VT)
+    group = second // VT
+
+    strip = local * NV + first
+    same = strip[:, None] == strip[None, :]
+    smaller = same & (second[None, :] < first[:, None])
+    here = same & (group[None, :] == vir)
+    rank_all = jnp.sum(smaller.astype(i32), axis=1)
+    which = jnp.sum((smaller & here).astype(i32), axis=1)
+    own_count = jnp.sum(here.astype(i32), axis=1)
+    together = group[:, None] == group[None, :]
+    rank_second = jnp.sum((same & together & (second[None, :] < second[:, None])).astype(i32), axis=1)
+    start = jnp.sum((together & (local[None, :] < local[:, None])).astype(i32), axis=1)
+
+    position = ((group - vir) % VIR) * VCAP + start + rank_second * own_count + which
+    own_map = lax.dynamic_slice_in_dim(cycle_map, occ * PAIRS, PAIRS, 0)
+    to_group = jnp.sum(
+        jnp.where(local[:, None] == jnp.arange(PAIRS, dtype=i32)[None, :], (own_map[None, :] - occ) % OCC, 0), axis=1
+    )
+    target = to_group * 16 + rank_second * 8 + rank_all
+    label = target + 256 * (first * 8 + second % VT)
     pick = jnp.arange(VIR * VCAP, dtype=i32)[:, None] == position[None, :]
     packed_pick = jnp.sum(jnp.where(pick, label * 128 + jnp.arange(128, dtype=i32) + 1, 0), axis=1)
     v_pack = jnp.where(packed_pick > 0, (packed_pick - 1) % 128, 0)
@@ -407,29 +413,23 @@
     tile_key = (local * 2 + which) * NV + second
     row_key = (ladder_slots[:, 0][None, :] * 2 + pair_range[:, None]) * NV + ladder_slots[:, 2][None, :]
     match = row_key[:, :, None] == tile_key[None, None, :]
-    packed = jnp.arange(128, dtype=i32) * 8 + first + 1
+    packed = jnp.arange(128, dtype=i32) * 8 + first - vir * VT + 1
     found = jnp.sum(jnp.where(match, packed, 0), axis=-1)
     ladder_tile = jnp.where(found > 0, (found - 1) // 8, 0)
     x_row = ladder_slots[:, 1]
     x_block = (ahead(x_row // 3) * 3 + x_row % 3) * VT
     ladder_block = jnp.where(found > 0, x_block[None, :] + (found - 1) % 8, BLOCKS)
 
-    by_o = (cycle_map.reshape(OCC, PAIRS) == occ).astype(i32)
-    ahead_of = jnp.sum(by_o * ((jnp.arange(OCC, dtype=i32) - occ) % OCC)[:, None], axis=0)
     s, a, b = cycle_slots[:, 0], cycle_slots[:, 1], cycle_slots[:, 2]
-    rows = jnp.stack([lookup(s, ahead_of), a, ahead(b // 3) * 18 + b % 3], axis=0)
+    pairs = jnp.arange(OCC * PAIRS, dtype=i32)
+    owned = (cycle_map[None, :] == occ) & (pairs[None, :] % PAIRS == s[:, None])
+    ahead_of = jnp.sum(jnp.where(owned, (pairs // PAIRS - occ) % OCC, 0), axis=1)
+    rows = jnp.stack([ahead_of, a, ahead(b // 3) * 18 + b % 3], axis=0)
     rows = jnp.pad(rows, ((0, 5), (0, 256 - ROWS)), constant_values=-1).reshape(8, 2, 128).transpose(1, 0, 2)
 
     index = jnp.concatenate([v_pack, ladder_block.reshape(-1), ladder_tile.reshape(-1)])
-    x_flat = jnp.concatenate([x_ints[:FLAT], x_ints[FLAT:]], axis=1)
-    y_rows = y_ints.reshape(3, 2, TILE, 3, TILE).transpose(0, 2, 1, 3, 4).reshape(3 * TILE, 6 * TILE)
-    y_flat = jnp.concatenate([y_rows[:FLAT], y_rows[FLAT:]], axis=1)
-    ladder, cycle = main_call(index, labels, rows, t_tiles.reshape(128, TILE, TILE), x_flat, y_flat)
-
-    def finish(octets):
-        return octets.reshape(3, TILE, 8, TILE).transpose(0, 2, 1, 3).reshape(24, AREA)
-
-    return finish(ladder), finish(cycle)
+    ladder, cycle = main_call(index, labels, rows, t_tiles.reshape(128, TILE, TILE), x_ints, y_ints)
+    return ladder.reshape(24, AREA), cycle.reshape(24, AREA)
 
 
 def solution(mesh):

time: 205 us -> 184 us (0.90)
  Pallas kernels: 176 us -> 158 us
    pallas_call x1, Pallas kernels: 176 us -> 158 us  [main_call(): pl.pallas_call(main_kernel, out_shape=(out, out), in_specs=[pl.BlockSpec(...]
    reshape x8 -> x2, local copies, waits for them, and re-layouts: 7.46 us -> 4.57 us  [on_device(): return (ladder.reshape(24, AREA), cycle.reshape(24, AREA))]
    another operation x4 -> x1, other arithmetic: 2.73 us -> 0.01 us  [on_device(): rows = jnp.stack([ahead_of, a, ahead(b // 3) * 18 + b % 3], axis=0)]
    unnamed x11 -> x4, local copies, waits for them, and re-layouts: 3.06 us -> 4.98 us
where the time goes in v4:
time: 184 us; the launch traced here: 182 us
  Pallas kernels  158 us (86%)
  local copies, waits for them, and re-layouts  15.3 us (8%)
  other arithmetic  8.32 us (5%)
    pallas_call x1, Pallas kernels, main_call(): pl.pallas_call(main_kernel, out_shape=(out, out), in_specs=[pl.BlockSpec(...  158 us
    unnamed x4, local copies, waits for them, and re-layouts  4.98 us
    reshape x2, local copies, waits for them, and re-layouts, on_device(): return (ladder.reshape(24, AREA), cycle.reshape(24, AREA))  4.57 us

profile of v4, /device:TPU:28, one launch (start us, length us, event | category | flops | bytes accessed | tf_op | source)
XLA Modules:
  0.0 181.8 jit_solution(3167062656592884760)
XLA Ops:
  0.7 0.8 and_select_fusion.16
  1.4 0.7 broadcast_compare_fusion.2
  2.1 0.7 compare_reduce_fusion
  2.8 0.7 fusion.13
  3.5 0.7 broadcast_compare_fusion.4
  4.3 0.8 fusion.36
  5.1 0.1 select_reduce_fusion.3
  5.2 0.7 multiply_add_fusion.2
  5.8 0.3 convert_reduce_fusion
  6.1 0.8 add_add_fusion
  6.9 0.1 select_reduce_fusion.2
  7.0 0.1 gt.23
  7.1 0.8 fusion.38
  7.9 0.2 select_reduce_fusion
  8.1 0.6 pad_bitcast_fusion.rows_ref
  8.7 0.1 sub.176
  8.8 0.8 broadcast_divide_fusion
  9.7 0.1 add.373
  9.8 0.2 select_reduce_fusion.1
  10.0 0.1 gt.22
  10.1 0.1 sub.174
  10.2 0.6 pad_add_fusion.index_ref
  10.8 0.8 broadcast_in_dim.74.label_ref
  11.6 1.9 %copy.15.y_ref = bf16[576,288]{1,0:T(8,128)(2,1)} copy(bf16[576,288]{0,1:T(8,128)(2,1)} %param.13) | data formatting | bytes 663552 | tf_op args[6]
  13.5 3.0 %copy.13 = bf16[128,9216]{0,1:T(8,128)(2,1)S(1)} copy(bf16[128,9216]{1,0:T(8,128)(2,1)} %param.7) | data formatting | bytes 4718592 | tf_op args[0]
  16.5 3.2 %copy.14.t_ref = bf16[128,96,96]{2,1,0:T(8,128)(2,1)} copy(bf16[128,96,96]{0,2,1:T(8,128)(2,1)S(1)} %bitcast.52) | data formatting | bytes 4718592 | tf_op jit(solution)/shard_map/reshape | solution.py:431
  19.7 157.5 %contract.1 = (f32[24,96,96]{2,1,0:T(8,128)}, f32[24,96,96]{2,1,0:T(8,128)}) custom-call(s32[1024]{0:T(1024)} %pad_add_fusion.index_ref, s32[8,32,128]{2,1,0:T(8,128)} %broadcast_in_dim.74.label_ref, s32[2,8,128]{2,1,0:T(8,128)} %pad_bitcast_fusion.rows_ref, bf16[128,96,96]{2,1,0:T(8,128)(2,1)} %copy.14.t_ref, bf16[288,576]{1,0:T(8,128)(2,1)} %x_ref.1, ...), custom_call_target="tpu_custom_call" | custom-call | flops 1358954496 | bytes 14000000 | tf_op jit(solution)/shard_map/contract/pallas_call | solution.py:333
  177.2 0.0 copy-start
  177.2 3.0 %reshape.510 = f32[24,9216]{1,0:T(8,128)} reshape(f32[24,96,96]{2,1,0:T(8,128)} %get-tuple-element.4) | data formatting | bytes 1769472 | tf_op jit(solution)/shard_map/reshape | solution.py:432
  180.2 0.0 copy-done
  180.2 1.6 reshape.511
  (10 shorter events, 0.1 us)
Async XLA Ops:
  177.2 3.0 %copy-start = (f32[24,96,96]{2,1,0:T(8,128)S(1)}, f32[24,96,96]{2,1,0:T(8,128)}, u32[]{:S(2)}) copy-start(f32[24,96,96]{2,1,0:T(8,128)} %get-tuple-element.5) | copy-start | bytes 2654212

commit v5 on v4

--- a/solution.py
+++ b/solution.py
@@ -49,10 +49,11 @@
         x_flat[:, part * 6 * TILE : (part + 1) * 6 * TILE] = x_ref[part * FLAT : (part + 1) * FLAT]
     for d in range(6):
         first_row, lane = (d // 2) * TILE, (d % 2) * 3 * TILE
+        strip = jnp.transpose(y_ref[:, d * TILE : (d + 1) * TILE])
         for start in range(0, TILE, 48):
             row = first_row + start
             shift = (row // FLAT) * 6 * TILE + lane
-            y_flat[row % FLAT : row % FLAT + 48, shift : shift + 3 * TILE] = y_ref[d * TILE + start : d * TILE + start + 48]
+            y_flat[row % FLAT : row % FLAT + 48, shift : shift + 3 * TILE] = strip[start : start + 48]
     pl.semaphore_wait(barrier, VIR + OCC - 2)
     sent = []
 
@@ -247,11 +248,11 @@
             for k in range(1, OCC)
         ]
 
-    def products(look, tiles, part, held, swap):
-        def octet(q, carry):
-            owner = q // 3
+    def products(look, tiles, part, held, swap, dest):
+        def octet(n, carry):
+            side, i = n // 3, n % 3
             for j in range(8):
-                row = q * 8 + j
+                row = ((dest * 2 + side) * 3 + i) * 8 + j
                 total = None
                 for half in range(2):
                     block = blocks[look(half, row)]
@@ -259,28 +260,40 @@
                     left, right = (tile, block) if swap else (block, tile)
                     term = jnp.dot(left, right, preferred_element_type=jnp.float32)
                     total = term if total is None else total + term
-                part[owner % 2, owner // 2, q % 3, held, j * TILE : (j + 1) * TILE] = total.astype(jnp.bfloat16)
+                part[side, dest, i, held, j * TILE : (j + 1) * TILE] = total.astype(jnp.bfloat16)
             return carry
 
-        lax.fori_loop(0, ROWS // 8, octet, 0)
-
-    def core_push(n, part, dst, held):
-        return push(part.at[1 - core, :, :, held], dst.at[:, :, held], core_ss.at[n], core_rs.at[n], (occ, z * 2 + 1 - core))
-
-    def z_push(n, copy, part, dst, z_got, held):
+        lax.fori_loop(0, 6, octet, 0)
+
+    def core_push(n, k, part, dst, held):
+        dest = (z + k) % 4
+        return push(
+            part.at[1 - core, dest, :, held], dst.at[dest, :, held],
+            core_ss.at[n, k], core_rs.at[n, k], (occ, z * 2 + 1 - core),
+        )
+
+    def z_push(n, k, copy, part, dst, z_got, held):
         copy.wait_recv()
-
-        def add(q, carry):
-            total = part[core, q // 3, q % 3, held].astype(jnp.float32) + dst[q // 3, q % 3, held].astype(jnp.float32)
-            dst[q // 3, q % 3, held] = total.astype(jnp.bfloat16)
-            return carry
-
-        lax.fori_loop(0, 12, add, 0)
-        return [
-            push(dst.at[(z + k) % 4, :, held], z_got.at[4 - k - 1, :, held], z_ss.at[n, k - 1], z_rs.at[n, 4 - k - 1],
-                 (occ, ((z + k) % 4) * 2 + core))
-            for k in (1, 3, 2)
-        ]
+        dest = (z + k) % 4
+        for i in range(3):
+            total = part[core, dest, i, held].astype(jnp.float32) + dst[dest, i, held].astype(jnp.float32)
+            dst[dest, i, held] = total.astype(jnp.bfloat16)
+        if k == 0:
+            return []
+        return [push(
+            dst.at[dest, :, held], z_got.at[4 - k - 1, :, held], z_ss.at[n, k - 1], z_rs.at[n, 4 - k - 1],
+            (occ, dest * 2 + core),
+        )]
+
+    def all_rows(n, look, tiles, part, dst, z_got, held, swap):
+        copies, before = [], None
+        for k in (2, 1, 3, 0):
+            products(look, tiles, part, held, swap, (z + k) % 4)
+            copy = core_push(n, k, part, dst, held)
+            if before is not None:
+                copies = copies + z_push(n, before[0], before[1], part, dst, z_got, held)
+            before = (k, copy)
+        return copies, before
 
     def finish(copies, dst, z_got, out, held):
         for copy in copies:
@@ -295,12 +308,13 @@
     whole = pl.ds(0, TILE)
     o_copies = [o_step(h) for h in range(H)]
     gather_unpack(0)
-    products(lambda n, row: index_ref[LADDER + n * ROWS + row], t_ref, l_part, whole, False)
-    l_copy = core_push(H, l_part, l_core, whole)
+    l_copies, rest = all_rows(
+        H, lambda n, row: index_ref[LADDER + n * ROWS + row], t_ref, l_part, l_core, l_z, whole, False
+    )
     cycle_words()
     gather_unpack(1)
-    l_copies = z_push(H, l_copy, l_part, l_core, l_z, whole)
-    c_copies = []
+    l_copies = l_copies + z_push(H, *rest, l_part, l_core, l_z, whole)
+    c_copies, rests = [], []
     for h in range(H):
         for copy in o_copies[h]:
             copy.wait_recv()
@@ -313,13 +327,14 @@
             return carry
 
         lax.fori_loop(0, (OCC - 1) * 2, unpack, 0)
-        products(lambda n, row: c_index[(row // 128) * 4 + n, row % 128], tiles, c_part, rows(h), True)
-        c_copies.append(core_push(h, c_part, c_core, rows(h)))
-        if h > 0:
-            c_copies[h - 1] = z_push(h - 1, c_copies[h - 1], c_part, c_core, c_z, rows(h - 1))
+        copies, rest = all_rows(
+            h, lambda n, row: c_index[(row // 128) * 4 + n, row % 128], tiles, c_part, c_core, c_z, rows(h), True
+        )
+        c_copies.append(copies)
+        rests.append(rest)
     finish(l_copies, l_core, l_z, ladder_ref, whole)
-    c_copies[H - 1] = z_push(H - 1, c_copies[H - 1], c_part, c_core, c_z, rows(H - 1))
     for h in range(H):
+        z_push(h, *rests[h], c_part, c_core, c_z, rows(h))
         finish(c_copies[h], c_core, c_z, cycle_ref, rows(h))
     for copy in sent:
         copy.wait_send()
@@ -361,7 +376,7 @@
             dma((2, 20)), dma((2, OCC - 1, 2)),
             dma((H, VIR - 1)), dma((H, VIR - 1)),
             dma((H, OCC - 1)), dma((H, OCC - 1)),
-            dma((H + 1,)), dma((H + 1,)),
+            dma((H + 1, 4)), dma((H + 1, 4)),
             dma((H + 1, 3)), dma((H + 1, 3)),
             dma((VIR - 1,)), dma((VIR - 1,)), dma((OCC - 1,)), dma((OCC - 1,)), dma((2,)),
         ],
@@ -428,7 +443,7 @@
     rows = jnp.pad(rows, ((0, 5), (0, 256 - ROWS)), constant_values=-1).reshape(8, 2, 128).transpose(1, 0, 2)
 
     index = jnp.concatenate([v_pack, ladder_block.reshape(-1), ladder_tile.reshape(-1)])
-    ladder, cycle = main_call(index, labels, rows, t_tiles.reshape(128, TILE, TILE), x_ints, y_ints)
+    ladder, cycle = main_call(index, labels, rows, t_tiles.reshape(128, TILE, TILE), x_ints, y_ints.T)
     return ladder.reshape(24, AREA), cycle.reshape(24, AREA)
 
 

time: 184 us -> 174 us (0.946)
  Pallas kernels: 158 us -> 150 us
  local copies, waits for them, and re-layouts: 15.3 us -> 13.3 us
    pallas_call x1, Pallas kernels: 158 us -> 150 us  [main_call(): pl.pallas_call(main_kernel, out_shape=(out, out), in_specs=[pl.BlockSpec(...]
    unnamed x4 -> x3, local copies, waits for them, and re-layouts: 4.98 us -> 3.04 us
where the time goes in v5:
time: 174 us; the launch traced here: 172 us
  Pallas kernels  150 us (86%)
  local copies, waits for them, and re-layouts  13.3 us (8%)
  other arithmetic  8.33 us (5%)
    pallas_call x1, Pallas kernels, main_call(): pl.pallas_call(main_kernel, out_shape=(out, out), in_specs=[pl.BlockSpec(...  150 us
    reshape x2, local copies, waits for them, and re-layouts, on_device(): return (ladder.reshape(24, AREA), cycle.reshape(24, AREA))  4.57 us

profile of v5, /device:TPU:28, one launch (start us, length us, event | category | flops | bytes accessed | tf_op | source)
XLA Modules:
  0.0 172.3 jit_solution(12038693976910530355)
XLA Ops:
  0.7 0.8 and_select_fusion.16
  1.4 0.7 broadcast_compare_fusion.2
  2.1 0.7 compare_reduce_fusion
  2.8 0.7 fusion.13
  3.5 0.7 broadcast_compare_fusion.4
  4.3 0.8 fusion.36
  5.1 0.1 select_reduce_fusion.3
  5.2 0.7 multiply_add_fusion.2
  5.8 0.3 convert_reduce_fusion
  6.1 0.8 add_add_fusion
  6.9 0.1 select_reduce_fusion.2
  7.0 0.1 gt.23
  7.1 0.8 fusion.38
  7.9 0.2 select_reduce_fusion
  8.1 0.6 pad_bitcast_fusion.rows_ref
  8.7 0.1 sub.176
  8.8 0.8 broadcast_divide_fusion
  9.7 0.1 add.373
  9.8 0.2 select_reduce_fusion.1
  10.0 0.1 gt.22
  10.1 0.1 sub.174
  10.2 0.6 pad_add_fusion.index_ref
  10.8 0.8 broadcast_in_dim.74.label_ref
  11.6 3.0 %copy.11 = bf16[128,9216]{0,1:T(8,128)(2,1)S(1)} copy(bf16[128,9216]{1,0:T(8,128)(2,1)} %param.7) | data formatting | bytes 4718592 | tf_op args[0]
  14.6 3.2 %copy.12.t_ref = bf16[128,96,96]{2,1,0:T(8,128)(2,1)} copy(bf16[128,96,96]{0,2,1:T(8,128)(2,1)S(1)} %bitcast.53) | data formatting | bytes 4718592 | tf_op jit(solution)/shard_map/reshape | solution.py:446
  17.8 149.9 %contract.1 = (f32[24,96,96]{2,1,0:T(8,128)}, f32[24,96,96]{2,1,0:T(8,128)}) custom-call(s32[1024]{0:T(1024)} %pad_add_fusion.index_ref, s32[8,32,128]{2,1,0:T(8,128)} %broadcast_in_dim.74.label_ref, s32[2,8,128]{2,1,0:T(8,128)} %pad_bitcast_fusion.rows_ref, bf16[128,96,96]{2,1,0:T(8,128)(2,1)} %copy.12.t_ref, bf16[288,576]{1,0:T(8,128)(2,1)} %x_ref.1, ...), custom_call_target="tpu_custom_call" | custom-call | flops 1358954496 | bytes 14000000 | tf_op jit(solution)/shard_map/contract/pallas_call | solution.py:348
  167.7 0.0 copy-start
  167.7 3.0 %reshape.510 = f32[24,9216]{1,0:T(8,128)} reshape(f32[24,96,96]{2,1,0:T(8,128)} %get-tuple-element.4) | data formatting | bytes 1769472 | tf_op jit(solution)/shard_map/reshape | solution.py:447
  170.7 0.0 copy-done
  170.7 1.6 reshape.511
  (10 shorter events, 0.1 us)
Async XLA Ops:
  167.7 3.0 %copy-start = (f32[24,96,96]{2,1,0:T(8,128)S(1)}, f32[24,96,96]{2,1,0:T(8,128)}, u32[]{:S(2)}) copy-start(f32[24,96,96]{2,1,0:T(8,128)} %get-tuple-element.5) | copy-start | bytes 2654212

commit v6 on v5

--- a/solution.py
+++ b/solution.py
@@ -24,11 +24,11 @@
 FLAT = 144
 SUBS = ((0, 80), (80, 64))
 MESH = pl.DeviceIdType.MESH
-VPACK, LADDER = 0, 256
 
 
 def main_kernel(
-    index_ref, label_ref, rows_ref, t_ref, x_ref, y_ref, ladder_ref, cycle_ref,
+    list_ref, map_ref, rows_ref, t_ref, x_ref, y_ref, ladder_ref, cycle_ref,
+    index_ref, label_ref, first_words,
     x_flat, y_flat, x_got, y_got, blocks, v_send, v_got, o_send, o_got, small,
     l_part, l_core, l_z, c_part, c_core, c_z,
     v_label, o_label, o_label_got, words, o_index, c_index,
@@ -63,6 +63,61 @@
         sent.append(copy)
         return copy
 
+    def column(row):
+        return jnp.transpose(jnp.broadcast_to(row.astype(jnp.float32), (128, 128))).astype(i32)
+
+    def total(mask, value=1):
+        return jnp.sum(jnp.where(mask, value, 0), axis=0, keepdims=True)
+
+    def tile_words():
+        lane = lax.broadcasted_iota(i32, (128, 128), 1)
+        at = [jnp.broadcast_to(list_ref[:, n : n + 1], (128, 128)) for n in range(3)]
+        local, first, second = at[0] - occ * PAIRS, at[1], at[2]
+        group = (second * 43) >> 8
+        k_local, k_first, k_second = (jnp.transpose(v.astype(jnp.float32)).astype(i32) for v in (local, first, second))
+        k_group = (k_second * 43) >> 8
+        same = (local == k_local) & (first == k_first)
+        smaller = same & (second < k_first)
+        here = same & (group == vir)
+        together = group == k_group
+        rank_all, which, own_count = total(smaller), total(smaller & here), total(here)
+        rank_second = total(same & together & (second < k_second))
+        start = total(together & (local < k_local))
+        k_local, k_first, k_second, k_group = (v[0:1] for v in (k_local, k_first, k_second, k_group))
+
+        position = ((k_group - vir) & 7) * VCAP + start + rank_second * own_count + which
+        one = lax.broadcasted_iota(i32, (PAIRS, OCC), 1) == occ
+        ahead = (jnp.sum(jnp.where(one, map_ref[...], 0), axis=1, keepdims=True) - occ) & 15
+        to_group = total(lax.broadcasted_iota(i32, (PAIRS, 128), 0) == k_local, jnp.broadcast_to(ahead, (PAIRS, 128)))
+        label = to_group * 16 + rank_second * 8 + rank_all + 256 * (k_first * 8 + k_second - 6 * k_group)
+        places = column(position)
+        values = column(label * 128 + lane[0:1] + 1)
+        first_words[...] = jnp.zeros((16, 128), i32)
+        for half in range(2):
+            found = total(places == lane + 128 * half, values)
+            first_words[half : half + 1] = jnp.where(found > 0, (found - 1) & 127, 0)
+            went = column(jnp.where(found > 0, (found - 1) >> 7, -1))
+            label_ref[half * 4 : half * 4 + 4] = went.reshape(4, VCAP, 128)
+
+        keys = column((k_local * 2 + which) * NV + k_second)
+        values = column(lane[0:1] * 8 + k_first - vir * VT + 1)
+        for half in range(2):
+            s, a, b = (rows_ref[half, n : n + 1] for n in (3, 4, 5))
+            third = (a * 171) >> 9
+            base = (ring_ahead(third) * 3 + a - 3 * third) * VT
+            for j in range(2):
+                found = total(keys == (s * 2 + j) * NV + b, values)
+                block = jnp.where(found > 0, base + ((found - 1) & 7), BLOCKS)
+                tile = jnp.where(found > 0, (found - 1) >> 3, 0)
+                first_words[2 + half * 4 + j : 3 + half * 4 + j] = jnp.clip(block, 0, BLOCKS)
+                first_words[4 + half * 4 + j : 5 + half * 4 + j] = jnp.clip(tile, 0, 127)
+        copy = pltpu.make_async_copy(first_words, index_ref, w_sem.at[2])
+        copy.start()
+        copy.wait()
+
+    def ring_ahead(group):
+        return (((group >> 2) - ox) & 3) * 4 + (((group & 3) - oy) & 3)
+
     shards = (x_flat, y_flat)
     landing = (x_got, y_got)
     count = [0, 0]
@@ -104,16 +159,18 @@
 
     first_axis, second_axis = (1, 0), (0, 1)
     first = [spread(array, first_axis[array], 0) for array in range(2)]
+    second = [{0: spread(array, second_axis[array], 0)} for array in range(2)]
+    turned = [[], []]
+
+    tile_words()
     v_labels = [
         push(label_ref.at[k], v_label.at[VIR - k - 1], vl_ss.at[k - 1], vl_rs.at[VIR - k - 1], (occ, (vir + k) % VIR))
         for k in range(1, VIR)
     ]
-    second = [{0: spread(array, second_axis[array], 0)} for array in range(2)]
-    turned = [[], []]
 
     def v_pack(q, carry):
         for j in range(8):
-            tile = t_ref[index_ref[VPACK + q * 8 + j]]
+            tile = t_ref[index_ref[q // 16, (q % 16) * 8 + j]]
             v_send[q // 4, q % 4, :, j * TILE : (j + 1) * TILE] = tile
         return carry
 
@@ -171,10 +228,6 @@
         rel = step(step(0, first_axis[array], 1), first_axis[array], 1)
         second[array][rel] = spread(array, second_axis[array], rel)
     blocks[BLOCKS] = jnp.zeros((TILE, TILE), jnp.bfloat16)
-    for n in range(4):
-        for array in range(2):
-            rel = list(second[array])[n]
-            turned[array] = turned[array] + forward(array, second_axis[array], rel, second[array][rel], n % 2)
 
     def gather_unpack(array):
         for copy in turned[array]:
@@ -198,6 +251,11 @@
     def cycle_words():
         line16 = lax.broadcasted_iota(i32, (16, 128), 0)
         totals = [jnp.zeros((16, 128), i32)] * 2
+        o_line = lax.broadcasted_iota(i32, (PAIRS, OCC), 1)
+        from_group = jnp.sum(jnp.where(map_ref[...] == occ, (o_line - occ) & 15, 0), axis=1, keepdims=True)
+        from_group = jnp.broadcast_to(from_group, (PAIRS, 128))
+        pair_of = [total(line16 == rows_ref[half, 0:1], from_group) for half in range(2)]
+        live = [rows_ref[half, 0:1] >= 0 for half in range(2)]
         for k in range(OCC):
             if k == 0:
                 label = o_label[0]
@@ -206,12 +264,15 @@
                 label = o_label_got[k - 1]
             value = (line16 + k * 16) * 8 + ((label - 1) & 7) + 1
             for half in range(2):
-                hit = (label > 0) & (rows_ref[half, 0:1] == k) & (((label - 1) >> 3) == rows_ref[half, 1:2])
+                hit = (label > 0) & live[half] & (pair_of[half] == k) & (((label - 1) >> 3) == rows_ref[half, 1:2])
                 totals[half] = totals[half] + jnp.where(hit, value, 0)
         for half in range(2):
             for j in range(2):
                 found = jnp.sum(totals[half][j * 8 : j * 8 + 8], axis=0, keepdims=True)
-                block = jnp.where(found > 0, rows_ref[half, 2:3] + 3 * ((found - 1) & 7), BLOCKS)
+                b = rows_ref[half, 2:3]
+                third = (b * 171) >> 9
+                base = ring_ahead(third) * 18 + b - 3 * third
+                block = jnp.where(found > 0, base + 3 * ((found - 1) & 7), BLOCKS)
                 tile = jnp.where(found > 0, (found - 1) >> 3, 0)
                 words[8 + half * 4 + j : 9 + half * 4 + j] = jnp.clip(block, 0, BLOCKS)
                 words[10 + half * 4 + j : 11 + half * 4 + j] = jnp.minimum(tile, 255)
@@ -306,10 +367,17 @@
                 out[i * 8 + j, held] = total[:, j * TILE : (j + 1) * TILE]
 
     whole = pl.ds(0, TILE)
-    o_copies = [o_step(h) for h in range(H)]
+    o_copies = []
+    for n in range(4):
+        for array in range(2):
+            rel = list(second[array])[n]
+            turned[array] = turned[array] + forward(array, second_axis[array], rel, second[array][rel], n % 2)
+        if n == 1:
+            o_copies.append(o_step(0))
+    o_copies = o_copies + [o_step(h) for h in range(1, H)]
     gather_unpack(0)
     l_copies, rest = all_rows(
-        H, lambda n, row: index_ref[LADDER + n * ROWS + row], t_ref, l_part, l_core, l_z, whole, False
+        H, lambda n, row: index_ref[2 + (row // 128) * 4 + n, row % 128], t_ref, l_part, l_core, l_z, whole, False
     )
     cycle_words()
     gather_unpack(1)
@@ -340,7 +408,7 @@
         copy.wait_send()
 
 
-def main_call(index, labels, rows, tiles, x, y):
+def main_call(index, owners, rows, tiles, x, y):
     bf16 = jnp.bfloat16
     vmem = pl.BlockSpec(memory_space=pltpu.VMEM)
     dma = pltpu.SemaphoreType.DMA
@@ -348,9 +416,12 @@
     return pl.pallas_call(
         main_kernel,
         out_shape=(out, out),
-        in_specs=[pl.BlockSpec(memory_space=pltpu.SMEM)] + [vmem] * 5,
+        in_specs=[vmem] * 6,
         out_specs=(vmem, vmem),
         scratch_shapes=[
+            pltpu.SMEM((16, 128), jnp.int32),
+            pltpu.VMEM((VIR, VCAP, 128), jnp.int32),
+            pltpu.VMEM((16, 128), jnp.int32),
             pltpu.VMEM((FLAT, 12 * TILE), bf16),
             pltpu.VMEM((FLAT, 12 * TILE), bf16),
             pltpu.VMEM((OCC - 1, FLAT, 12 * TILE), bf16),
@@ -378,72 +449,21 @@
             dma((H, OCC - 1)), dma((H, OCC - 1)),
             dma((H + 1, 4)), dma((H + 1, 4)),
             dma((H + 1, 3)), dma((H + 1, 3)),
-            dma((VIR - 1,)), dma((VIR - 1,)), dma((OCC - 1,)), dma((OCC - 1,)), dma((2,)),
+            dma((VIR - 1,)), dma((VIR - 1,)), dma((OCC - 1,)), dma((OCC - 1,)), dma((3,)),
         ],
         compiler_params=pltpu.CompilerParams(
             collective_id=1, has_side_effects=True, vmem_limit_bytes=63_000_000
         ),
         cost_estimate=pl.CostEstimate(flops=8 * ROWS * TILE**3, bytes_accessed=14_000_000, transcendentals=0),
         name="contract",
-    )(index, labels, rows, tiles, x, y)
+    )(index, owners, rows, tiles, x, y)
 
 
 def on_device(t_tiles, t_index, cycle_map, ladder_slots, cycle_slots, x_ints, y_ints):
-    occ = lax.axis_index("occ")
-    vir = lax.axis_index("vir")
-    i32 = jnp.int32
-    pair_range = jnp.arange(2, dtype=i32)
-    local = t_index[:, 0] - occ * PAIRS
-    first = t_index[:, 1]
-    second = t_index[:, 2]
-    group = second // VT
-
-    strip = local * NV + first
-    same = strip[:, None] == strip[None, :]
-    smaller = same & (second[None, :] < first[:, None])
-    here = same & (group[None, :] == vir)
-    rank_all = jnp.sum(smaller.astype(i32), axis=1)
-    which = jnp.sum((smaller & here).astype(i32), axis=1)
-    own_count = jnp.sum(here.astype(i32), axis=1)
-    together = group[:, None] == group[None, :]
-    rank_second = jnp.sum((same & together & (second[None, :] < second[:, None])).astype(i32), axis=1)
-    start = jnp.sum((together & (local[None, :] < local[:, None])).astype(i32), axis=1)
-
-    position = ((group - vir) % VIR) * VCAP + start + rank_second * own_count + which
-    own_map = lax.dynamic_slice_in_dim(cycle_map, occ * PAIRS, PAIRS, 0)
-    to_group = jnp.sum(
-        jnp.where(local[:, None] == jnp.arange(PAIRS, dtype=i32)[None, :], (own_map[None, :] - occ) % OCC, 0), axis=1
-    )
-    target = to_group * 16 + rank_second * 8 + rank_all
-    label = target + 256 * (first * 8 + second % VT)
-    pick = jnp.arange(VIR * VCAP, dtype=i32)[:, None] == position[None, :]
-    packed_pick = jnp.sum(jnp.where(pick, label * 128 + jnp.arange(128, dtype=i32) + 1, 0), axis=1)
-    v_pack = jnp.where(packed_pick > 0, (packed_pick - 1) % 128, 0)
-    labels = jnp.where(packed_pick > 0, (packed_pick - 1) // 128, -1)
-    labels = jnp.broadcast_to(labels.reshape(VIR, VCAP, 1), (VIR, VCAP, 128))
-
-    def ahead(group):
-        return ((group // 4 - occ // 4) % 4) * 4 + (group % 4 - occ % 4) % 4
-
-    tile_key = (local * 2 + which) * NV + second
-    row_key = (ladder_slots[:, 0][None, :] * 2 + pair_range[:, None]) * NV + ladder_slots[:, 2][None, :]
-    match = row_key[:, :, None] == tile_key[None, None, :]
-    packed = jnp.arange(128, dtype=i32) * 8 + first - vir * VT + 1
-    found = jnp.sum(jnp.where(match, packed, 0), axis=-1)
-    ladder_tile = jnp.where(found > 0, (found - 1) // 8, 0)
-    x_row = ladder_slots[:, 1]
-    x_block = (ahead(x_row // 3) * 3 + x_row % 3) * VT
-    ladder_block = jnp.where(found > 0, x_block[None, :] + (found - 1) % 8, BLOCKS)
-
-    s, a, b = cycle_slots[:, 0], cycle_slots[:, 1], cycle_slots[:, 2]
-    pairs = jnp.arange(OCC * PAIRS, dtype=i32)
-    owned = (cycle_map[None, :] == occ) & (pairs[None, :] % PAIRS == s[:, None])
-    ahead_of = jnp.sum(jnp.where(owned, (pairs // PAIRS - occ) % OCC, 0), axis=1)
-    rows = jnp.stack([ahead_of, a, ahead(b // 3) * 18 + b % 3], axis=0)
-    rows = jnp.pad(rows, ((0, 5), (0, 256 - ROWS)), constant_values=-1).reshape(8, 2, 128).transpose(1, 0, 2)
-
-    index = jnp.concatenate([v_pack, ladder_block.reshape(-1), ladder_tile.reshape(-1)])
-    ladder, cycle = main_call(index, labels, rows, t_tiles.reshape(128, TILE, TILE), x_ints, y_ints.T)
+    slots = jnp.concatenate([cycle_slots, ladder_slots], axis=1).T
+    rows = jnp.pad(slots, ((0, 2), (0, 256 - ROWS)), constant_values=-1).reshape(8, 2, 128).transpose(1, 0, 2)
+    owners = cycle_map.reshape(OCC, PAIRS).T
+    ladder, cycle = main_call(t_index, owners, rows, t_tiles.reshape(128, TILE, TILE), x_ints, y_ints.T)
     return ladder.reshape(24, AREA), cycle.reshape(24, AREA)
 
 

time: 174 us -> 170 us (0.977)
  other arithmetic: 8.33 us -> 0.71 us
  Pallas kernels: 150 us -> 152 us
    eq x3 -> x0, other arithmetic: 2.2 us -> none  [the longest x1 0.81 us: on_device(): together = group[:, None] == group[None, :]]
    add x4 -> x0, other arithmetic: 2.2 us -> none  [the longest x1 0.78 us: on_device(): label * 128 + jnp.arange(128, dtype=i32) + 1]
    pallas_call x1, Pallas kernels: 150 us -> 152 us  [main_call(): pl.pallas_call(main_kernel, out_shape=(out, out), in_specs=[vmem] * 6, ou...]
    unnamed x3 -> x4, local copies, waits for them, and re-layouts: 3.04 us -> 4.45 us
where the time goes in v6:
time: 170 us; the launch traced here: 168 us
  Pallas kernels  152 us (89%)
  local copies, waits for them, and re-layouts  14.2 us (8%)
    pallas_call x1, Pallas kernels, main_call(): pl.pallas_call(main_kernel, out_shape=(out, out), in_specs=[vmem] * 6, ou...  152 us
    reshape x2, local copies, waits for them, and re-layouts, on_device(): return (ladder.reshape(24, AREA), cycle.reshape(24, AREA))  4.57 us
    unnamed x4, local copies, waits for them, and re-layouts  4.45 us

profile of v6, /device:TPU:28, one launch (start us, length us, event | category | flops | bytes accessed | tf_op | source)
XLA Modules:
  0.0 167.5 jit_solution(10546592776098799047)
XLA Ops:
  0.6 0.8 reshape.19
  1.4 0.7 copy.10
  2.1 0.7 add_bitcast_fusion
  2.8 0.6 pad_bitcast_fusion.rows_ref
  3.4 1.4 copy.12.list_ref
  4.8 3.0 %copy.11 = bf16[128,9216]{0,1:T(8,128)(2,1)S(1)} copy(bf16[128,9216]{1,0:T(8,128)(2,1)} %param.7) | data formatting | bytes 4718592 | tf_op args[0]
  7.8 3.1 %copy.13.t_ref = bf16[128,96,96]{2,1,0:T(8,128)(2,1)} copy(bf16[128,96,96]{0,2,1:T(8,128)(2,1)S(1)} %bitcast.9) | data formatting | bytes 4718592 | tf_op jit(solution)/shard_map/reshape | solution.py:466
  10.9 152.0 %contract.1 = (f32[24,96,96]{2,1,0:T(8,128)}, f32[24,96,96]{2,1,0:T(8,128)}) custom-call(s32[128,3]{1,0:T(8,128)} %copy.12.list_ref, s32[16,16]{1,0:T(8,128)} %bitcast.10, s32[2,8,128]{2,1,0:T(8,128)} %pad_bitcast_fusion.rows_ref, bf16[128,96,96]{2,1,0:T(8,128)(2,1)} %copy.13.t_ref, bf16[288,576]{1,0:T(8,128)(2,1)} %x_ref.1, bf16[288,576]{1,0:T(8,128)(2,1)} %bitcast.11), custom_call_target="tpu_custom_call" | custom-call | flops 1358954496 | bytes 14000000 | tf_op jit(solution)/shard_map/contract/pallas_call | solution.py:416
  162.9 0.0 copy-start
  163.0 3.0 %reshape.22 = f32[24,9216]{1,0:T(8,128)} reshape(f32[24,96,96]{2,1,0:T(8,128)} %get-tuple-element.4) | data formatting | bytes 1769472 | tf_op jit(solution)/shard_map/reshape | solution.py:467
  165.9 0.0 copy-done
  165.9 1.6 reshape.23
Async XLA Ops:
  162.9 3.0 %copy-start = (f32[24,96,96]{2,1,0:T(8,128)S(1)}, f32[24,96,96]{2,1,0:T(8,128)}, u32[]{:S(2)}) copy-start(f32[24,96,96]{2,1,0:T(8,128)} %get-tuple-element.5) | copy-start | bytes 2654212

commit v7 on v6

--- a/solution.py
+++ b/solution.py
@@ -306,7 +306,7 @@
         return [
             push(o_send.at[k, :, rows(h)], o_got.at[OCC - k - 1, :, rows(h)], o_ss.at[h, k - 1],
                  o_rs.at[h, OCC - k - 1], ((occ + k) % OCC, vir))
-            for k in range(1, OCC)
+            for k in (10, 6, 14, 9, 11, 2, 8, 5, 7, 13, 15, 1, 3, 4, 12)
         ]
 
     def products(look, tiles, part, held, swap, dest):

time: 170 us -> 167 us (0.982)
  the two profiles are of different devices: /device:TPU:28 before, /device:TPU:16 now
where the time goes in v7:
time: 167 us
  Pallas kernels  151 us (90%)
  local copies, waits for them, and re-layouts  14.2 us (9%)
    pallas_call x1, Pallas kernels, main_call(): pl.pallas_call(main_kernel, out_shape=(out, out), in_specs=[vmem] * 6, ou...  151 us
    reshape x2, local copies, waits for them, and re-layouts, on_device(): return (ladder.reshape(24, AREA), cycle.reshape(24, AREA))  4.57 us
    unnamed x4, local copies, waits for them, and re-layouts  4.45 us

profile of v7, /device:TPU:16, one launch (start us, length us, event | category | flops | bytes accessed | tf_op | source)
XLA Modules:
  0.0 166.5 jit_solution(12454646547084228118)
XLA Ops:
  0.6 0.8 reshape.19
  1.4 0.7 copy.10
  2.1 0.7 add_bitcast_fusion
  2.8 0.6 pad_bitcast_fusion.rows_ref
  3.4 1.4 copy.12.list_ref
  4.8 3.0 %copy.11 = bf16[128,9216]{0,1:T(8,128)(2,1)S(1)} copy(bf16[128,9216]{1,0:T(8,128)(2,1)} %param.7) | data formatting | bytes 4718592 | tf_op args[0]
  7.8 3.1 %copy.13.t_ref = bf16[128,96,96]{2,1,0:T(8,128)(2,1)} copy(bf16[128,96,96]{0,2,1:T(8,128)(2,1)S(1)} %bitcast.9) | data formatting | bytes 4718592 | tf_op jit(solution)/shard_map/reshape | solution.py:466
  10.9 151.0 %contract.1 = (f32[24,96,96]{2,1,0:T(8,128)}, f32[24,96,96]{2,1,0:T(8,128)}) custom-call(s32[128,3]{1,0:T(8,128)} %copy.12.list_ref, s32[16,16]{1,0:T(8,128)} %bitcast.10, s32[2,8,128]{2,1,0:T(8,128)} %pad_bitcast_fusion.rows_ref, bf16[128,96,96]{2,1,0:T(8,128)(2,1)} %copy.13.t_ref, bf16[288,576]{1,0:T(8,128)(2,1)} %x_ref.1, bf16[288,576]{1,0:T(8,128)(2,1)} %bitcast.11), custom_call_target="tpu_custom_call" | custom-call | flops 1358954496 | bytes 14000000 | tf_op jit(solution)/shard_map/contract/pallas_call | solution.py:416
  162.0 0.0 copy-start
  162.0 3.0 %reshape.22 = f32[24,9216]{1,0:T(8,128)} reshape(f32[24,96,96]{2,1,0:T(8,128)} %get-tuple-element.4) | data formatting | bytes 1769472 | tf_op jit(solution)/shard_map/reshape | solution.py:467
  164.9 0.0 copy-done
  164.9 1.6 reshape.23
Async XLA Ops:
  162.0 3.0 %copy-start = (f32[24,96,96]{2,1,0:T(8,128)S(1)}, f32[24,96,96]{2,1,0:T(8,128)}, u32[]{:S(2)}) copy-start(f32[24,96,96]{2,1,0:T(8,128)} %get-tuple-element.5) | copy-start | bytes 2654212
